TPU v7x, 128 devices: a whole 4x4x4 slice. The times are simulated.
128 devices in a mesh: lat: 4 (over z), lon: 32 (over y, x, core).
Axes of the slice: x: 4, y: 4, z: 4, core: 2. Of those that a mesh axis runs over, the one named last changes fastest.
Arguments:
- latents: bfloat16 [32768, 512], P(('lat', 'lon')), may hold values from -6 to 6
- near_index: int32 [4, 32768], P(None, ('lat', 'lon')), may hold values from 0 to 511
- coarse_slot: int32 [2, 32768], P(None, ('lat', 'lon')), may hold values from 0 to 1023, as said below
- coarse_send: int32 [128, 1024], P(('lat', 'lon')), may hold values from 0 to 255
- norm_gain: float32 [512], replicated, may hold values from 0.1 to 1.9
- send_weight: bfloat16 [512, 512], replicated, may hold values from -0.25 to 0.25
- receive_weight: bfloat16 [512, 512], replicated, may hold values from -0.25 to 0.25
- edge_bias: float32 [512], replicated, may hold values from -3 to 3
- edge_weight: bfloat16 [512, 512], replicated, may hold values from -0.25 to 0.25
- edge_gain: float32 [512], replicated, may hold values from 0.1 to 1.9
- node_input: bfloat16 [1024, 512], replicated, may hold values from -0.1875 to 0.1875
- node_bias: float32 [512], replicated, may hold values from -3 to 3
- node_output: bfloat16 [512, 512], replicated, may hold values from -0.25 to 0.25
- cotangent: bfloat16 [32768, 512], P(('lat', 'lon')), may hold values from -6 to 6
Outputs:
- new_latents: bfloat16 [32768, 512], P(('lat', 'lon'))
- grad_latents: bfloat16 [32768, 512], P(('lat', 'lon'))
- grad_send: float32 [512, 512], replicated
- grad_receive: float32 [512, 512], replicated
- grad_edge: float32 [512, 512], replicated
- grad_node_input: float32 [1024, 512], replicated
- grad_node_output: float32 [512, 512], replicated
- grad_vectors: float32 [4, 512], replicated
Inputs may be any that keep to these rules, and one draw needn't show every extreme that they name: `coarse_slot`: on each device the 512 coarse edges name distinct slots. Slot s is position s % 8 among the rows that source device s // 8 (lat-major) sends to this device, so at most 8 of one device's coarse edges come from one source device.
All inputs are finite; a program needn't handle non-finite values.
Results may differ from a plain program's by a relative error of at most 0.012.
Values may be sent and summed in bfloat16 or wider, within the bound.
A program may use at most 64 MiB of HBM per device.

v0:
```python
import jax
import jax.numpy as jnp
from jax import lax
from jax.sharding import PartitionSpec as P

DEG = 4
RIM = 128


EPS = 1e-05


def padded(value, sides, width):
    for axis, dim in sides:
        devices, length = (lax.axis_size(axis), value.shape[dim])
        up = [(i, (i + 1) % devices) for i in range(devices)]
        down = [(j, i) for i, j in up]
        last = lax.slice_in_dim(value, length - width, length, axis=dim)
        first = lax.slice_in_dim(value, 0, width, axis=dim)
        before = lax.ppermute(last, axis, up)
        after = lax.ppermute(first, axis, down)
        value = jnp.concatenate([before, value, after], axis=dim)
    return value


def norm_rows(values):
    centred = values - jnp.mean(values, axis=-1, keepdims=True)
    inverse = lax.rsqrt(jnp.mean(centred * centred, axis=-1, keepdims=True) + EPS)
    return (centred * inverse, inverse)


def norm_back(upstream, normalized, inverse):
    return (
        upstream
        - jnp.mean(upstream, axis=-1, keepdims=True)
        - normalized * jnp.mean(upstream * normalized, axis=-1, keepdims=True)
    ) * inverse


def silu_slope(values):
    logistic = jax.nn.sigmoid(values)
    return logistic * (1.0 + values * (1.0 - logistic))


def outer_sum(former, latter):
    return lax.dot_general(
        former, latter, (((0,), (0,)), ((), ())), preferred_element_type=jnp.float32
    )


def back_dot(former, latter):
    return lax.dot_general(
        former, latter, (((1,), (1,)), ((), ())), preferred_element_type=jnp.float32
    )


def edge_node_pass(
    latents,
    normed,
    receive_part,
    senders,
    receive_weight,
    edge_weight,
    edge_gain,
    node_input,
    node_bias,
    node_output,
    cotangent,
):
    edge_count, row_count, feature = senders.shape
    edge_in = senders.astype(jnp.float32) + receive_part[None]
    activated = jax.nn.silu(edge_in).astype(jnp.bfloat16)
    flat_active = activated.reshape(edge_count * row_count, feature)
    edge_pre = jnp.dot(flat_active, edge_weight, preferred_element_type=jnp.float32)
    edge_hat, edge_inv = norm_rows(edge_pre)
    edge_hat = edge_hat.reshape(edge_count, row_count, feature)
    edge_inv = edge_inv.reshape(edge_count, row_count, 1)
    aggregate = jnp.sum(edge_hat * edge_gain, axis=0).astype(jnp.bfloat16)
    self_weight = node_input[:feature]
    other_weight = node_input[feature:]
    node_pre = (
        jnp.dot(normed, self_weight, preferred_element_type=jnp.float32)
        + jnp.dot(aggregate, other_weight, preferred_element_type=jnp.float32)
        + node_bias
    )
    hidden_units = jax.nn.silu(node_pre).astype(jnp.bfloat16)
    new_latents = (
        latents.astype(jnp.float32)
        + jnp.dot(hidden_units, node_output, preferred_element_type=jnp.float32)
    ).astype(jnp.bfloat16)
    grad_hidden = back_dot(cotangent, node_output)
    grad_node_pre = (grad_hidden * silu_slope(node_pre)).astype(jnp.bfloat16)
    grad_aggregate = back_dot(grad_node_pre, other_weight)
    grad_edge_pre = norm_back((grad_aggregate * edge_gain)[None], edge_hat, edge_inv).astype(
        jnp.bfloat16
    )
    flat_grad_pre = grad_edge_pre.reshape(edge_count * row_count, feature)
    grad_edge_in = back_dot(flat_grad_pre, edge_weight).reshape(
        edge_count, row_count, feature
    ) * silu_slope(edge_in)
    grad_receive = jnp.sum(grad_edge_in, axis=0).astype(jnp.bfloat16)
    grad_normed = back_dot(grad_node_pre, self_weight) + back_dot(grad_receive, receive_weight)
    matrices = (
        outer_sum(flat_active, flat_grad_pre),
        outer_sum(normed, grad_receive),
        jnp.concatenate(
            [outer_sum(normed, grad_node_pre), outer_sum(aggregate, grad_node_pre)], axis=0
        ),
        outer_sum(hidden_units, cotangent),
    )
    vectors = (
        jnp.sum(grad_edge_in, axis=(0, 1)),
        jnp.sum(grad_aggregate[None] * edge_hat, axis=(0, 1)),
        jnp.sum(grad_node_pre.astype(jnp.float32), axis=0),
    )
    return (new_latents, grad_normed, grad_edge_in, matrices, vectors)


def per_device(
    latents,
    near_index,
    coarse_slot,
    coarse_send,
    norm_gain,
    send_weight,
    receive_weight,
    edge_bias,
    edge_weight,
    edge_gain,
    node_input,
    node_bias,
    node_output,
    cotangent,
):
    row_count, feature = latents.shape
    lat_count = lax.axis_size("lat")
    lon_count = lax.axis_size("lon")
    slot_count = coarse_send.shape[1]
    latent_hat, latent_inv = norm_rows(latents.astype(jnp.float32))
    normed = (latent_hat * norm_gain).astype(jnp.bfloat16)
    sent = jnp.dot(normed, send_weight, preferred_element_type=jnp.float32).astype(jnp.bfloat16)
    receive_part = jnp.dot(normed, receive_weight, preferred_element_type=jnp.float32) + edge_bias
    extended = padded(sent, (("lon", 0),), RIM)
    send_rows = coarse_send[0]
    packed = sent[send_rows]
    arrived = lax.all_to_all(packed, ("lat", "lon"), split_axis=0, concat_axis=0, tiled=True)
    senders = jnp.concatenate([extended[near_index], arrived[coarse_slot]], axis=0)
    new_latents, grad_normed, grad_edge_in, matrices, vectors = edge_node_pass(
        latents,
        normed,
        receive_part,
        senders,
        receive_weight,
        edge_weight,
        edge_gain,
        node_input,
        node_bias,
        node_output,
        cotangent,
    )
    grad_extended = (
        jnp.zeros((row_count + 2 * RIM, feature), jnp.float32)
        .at[near_index.reshape(-1)]
        .add(grad_edge_in[:DEG].reshape(-1, feature))
    )
    rim_parts = jnp.concatenate([grad_extended[:RIM], grad_extended[RIM + row_count :]], axis=0)
    returned_rim = padded(rim_parts.astype(jnp.bfloat16), (("lon", 0),), RIM).astype(
        rim_parts.dtype
    )
    grad_sent = grad_extended[RIM : RIM + row_count]
    grad_sent = grad_sent.at[:RIM].add(returned_rim[:RIM])
    grad_sent = grad_sent.at[row_count - RIM :].add(returned_rim[3 * RIM :])
    bucket = (
        jnp.zeros((slot_count, feature), jnp.float32)
        .at[coarse_slot.reshape(-1)]
        .set(grad_edge_in[DEG:].reshape(-1, feature))
    )
    returned = lax.all_to_all(
        bucket.astype(jnp.bfloat16), ("lat", "lon"), split_axis=0, concat_axis=0, tiled=True
    ).astype(bucket.dtype)
    grad_sent = grad_sent.at[send_rows].add(returned).astype(jnp.bfloat16)
    grad_normed = grad_normed + back_dot(grad_sent, send_weight)
    grad_latents = (
        cotangent.astype(jnp.float32) + norm_back(grad_normed * norm_gain, latent_hat, latent_inv)
    ).astype(jnp.bfloat16)
    local_vectors = jnp.stack(
        [jnp.sum(grad_normed * latent_hat, axis=0), vectors[0], vectors[1], vectors[2]]
    )
    totals = lax.psum(
        (
            outer_sum(normed, grad_sent),
            matrices[1],
            matrices[0],
            matrices[2],
            matrices[3],
            local_vectors,
        ),
        ("lat", "lon"),
    )
    scale = float(row_count * lat_count * lon_count) ** (-0.5)
    return (
        new_latents,
        grad_latents,
        totals[0] * scale,
        totals[1] * scale,
        totals[2] * scale,
        totals[3] * scale,
        totals[4] * scale,
        totals[5] * scale,
    )


def solution(mesh):
    return jax.shard_map(
        per_device,
        mesh=mesh,
        in_specs=(
            P(("lat", "lon"), None),
            P(None, ("lat", "lon")),
            P(None, ("lat", "lon")),
            P(("lat", "lon"), None),
            P(),
            P(),
            P(),
            P(),
            P(),
            P(),
            P(),
            P(),
            P(),
            P(("lat", "lon"), None),
        ),
        out_specs=(P(("lat", "lon"), None), P(("lat", "lon"), None), P(), P(), P(), P(), P(), P()),
        check_vma=False,
    )
```

profile of v0, /device:TPU:1, one launch (start us, length us, event | category | flops | bytes accessed | tf_op | source)
XLA Modules:
  0.0 295.9 jit_solution(16528355466290137518)
XLA Ops:
  7.2 1.1 convert_reduce_fusion
  8.3 1.2 fusion.34
  9.5 1.5 convolution_convert_fusion
  11.0 2.7 collective-permute-start
  13.7 0.7 compare_select_fusion.1
  14.4 0.6 copy-done.35
  15.0 5.1 %gather_fusion.1 = bf16[1024,512]{1,0:T(8,128)(2,1)} fusion(bf16[256,512]{1,0:T(8,128)(2,1)S(1)} %convolution_convert_fusion, s32[1024]{0:T(1024)S(1)} %broadcast_clamp_fusion), kind=kCustom, calls=%fused_computation.1 | custom fusion | bytes 2101248 | tf_op jit(solution)/shard_map/gather | solution.py:145
  20.1 10.6 %all-to-all-start = ((bf16[128,8,512]{2,1,0:T(8,128)(2,1)}), bf16[128,8,512]{2,1,0:T(8,128)(2,1)S(1)}, u32[]{:S(2)}, u32[]{:S(2)}) async-start(bf16[128,8,512]{2,1,0:T(8,128)(2,1)} %bitcast.3), calls=%async_computation | async-start | bytes 2097152 | tf_op jit(solution)/shard_map/all_to_all | solution.py:146
  30.8 0.7 copy.26
  31.5 0.6 compare_select_fusion
  32.1 0.7 fusion.57
  32.8 0.7 copy.27
  33.5 1.1 fusion.43
  34.6 2.2 convolution_add_fusion.4
  36.8 0.5 compare_select_fusion.2
  37.4 0.6 pad_clamp_fusion
  38.0 0.9 pad_maximum_fusion.1
  38.9 5.1 %gather_fusion = bf16[1024,512]{1,0:T(8,128)(2,1)} fusion(bf16[512,512]{1,0:T(8,128)(2,1)S(1)} %pad_maximum_fusion.1, s32[1024]{0:T(1024)S(1)} %broadcast_clamp_fusion.1), kind=kCustom, calls=%fused_computation | custom fusion | bytes 2101248 | tf_op jit(solution)/shard_map/gather | solution.py:147
  44.0 6.1 %all-to-all-done = bf16[128,8,512]{2,1,0:T(8,128)(2,1)S(1)} async-done(((bf16[128,8,512]{2,1,0:T(8,128)(2,1)}), bf16[128,8,512]{2,1,0:T(8,128)(2,1)S(1)}, u32[]{:S(2)}, u32[]{:S(2)}) %all-to-all-start) | async-done | bytes 1048608 | tf_op jit(solution)/shard_map/all_to_all | solution.py:146
  50.1 2.6 gather_fusion.2
  52.7 1.6 convert_add_fusion
  54.4 0.9 fusion.7
  55.2 1.1 fusion.71
  56.3 0.6 multiply_reduce_fusion.1
  56.9 0.5 subtract_multiply_fusion
  57.6 0.4 multiply_reduce_fusion
  58.0 1.4 copy-done.14
  59.4 0.5 copy-done.29
  60.2 1.0 convert_reduce_fusion.1
  61.2 0.4 fusion.68
  61.8 1.0 fusion
  62.8 0.7 fusion.3
  64.0 5.6 %fusion.67 = (f32[512]{0:T(512)}, bf16[256,512]{1,0:T(8,128)(2,1)}, f32[6,256,512]{2,1,0:T(8,128)S(1)}) fusion(f32[256,512]{1,0:T(8,128)S(1)} %copy-done.24, bf16[2,256,512]{2,1,0:T(8,128)(2,1)S(1)} %bitcast.100, bf16[4,256,512]{2,1,0:T(8,128)(2,1)S(1)} %bitcast.96, bf16[6,256,512]{2,1,0:T(8,128)(2,1)S(1)} %bitcast.102, bf16[512,512]{1,0:T(8,128)(2,1)S(1)} %copy-done), kind=kOutput, calls=%fused_computation.126 | convolution fusion | flops 816971264 | bytes 7604224 | tf_op jit(solution)/shard_map/dot_general | solution.py:52
  69.6 1.5 slice.97
  71.1 1.0 slice.103
  72.2 1.4 fusion.60
  73.6 0.6 div.52
  74.2 0.6 rsqrt.26
  74.8 7.7 %scatter_custom_fusion = f32[512,512]{1,0:T(8,128)S(1)} fusion(s32[1024]{0:T(1024)} %bitcast.114, f32[1024,512]{1,0:T(8,128)} %bitcast.101, f32[]{:T(128)} %constant.89.clone.1), kind=kCustom, calls=%fused_computation.73 | custom fusion | flops 524288 | bytes 1049088 | tf_op jit(solution)/shard_map/scatter-add | solution.py:164
  82.6 0.8 fusion.69
  83.4 1.1 collective-permute-start.2
  84.5 3.4 %scatter_custom_fusion.1 = f32[1024,512]{1,0:T(8,128)S(1)} fusion(s32[512]{0:T(512)} %bitcast.115, f32[512,512]{1,0:T(8,128)} %bitcast.103, f32[]{:T(128)} %constant.89.clone.1), kind=kCustom, calls=%fused_computation.48 | custom fusion | bytes 2097664 | tf_op jit(solution)/shard_map/scatter | solution.py:176
  87.9 1.1 convert_bitcast_fusion
  89.0 8.4 %all-to-all-start.1 = ((bf16[128,8,512]{2,1,0:T(8,128)(2,1)}), bf16[128,8,512]{2,1,0:T(8,128)(2,1)S(1)}, u32[]{:S(2)}, u32[]{:S(2)}) async-start(bf16[128,8,512]{2,1,0:T(8,128)(2,1)} %convert_bitcast_fusion), calls=%async_computation.1 | async-start | bytes 2097152 | tf_op jit(solution)/shard_map/all_to_all | solution.py:178
  97.5 2.4 fusion.50
  99.9 5.0 %fusion.14 = f32[512,512]{1,0:T(8,128)} fusion(f32[6,256,512]{2,1,0:T(8,128)} %bitcast.94, f32[6,256]{1,0:T(8,128)} %rsqrt.26, f32[6,256]{1,0:T(8,128)} %div.52, f32[256,512]{1,0:T(8,128)} %copy-done.17, bf16[2,256,512]{2,1,0:T(8,128)(2,1)} %bitcast.99, bf16[4,256,512]{2,1,0:T(8,128)(2,1)S(1)} %bitcast.97, f32[256,512]{1,0:T(8,128)} %convolution_add_fusion.4), kind=kOutput, calls=%fused_computation.34 | convolution fusion | flops 814743552 | bytes 6828032 | tf_op jit(solution)/shard_map/dot_general | solution.py:46
  105.3 1.3 fusion.59
  106.6 1.5 pad_maximum_fusion
  108.1 0.9 fusion.46
  109.1 1.0 fusion.45
  110.0 6.9 %all-to-all-done.1 = bf16[128,8,512]{2,1,0:T(8,128)(2,1)S(1)} async-done(((bf16[128,8,512]{2,1,0:T(8,128)(2,1)}), bf16[128,8,512]{2,1,0:T(8,128)(2,1)S(1)}, u32[]{:S(2)}, u32[]{:S(2)}) %all-to-all-start.1) | async-done | bytes 1048608 | tf_op jit(solution)/shard_map/all_to_all | solution.py:178
  117.0 7.3 %scatter_custom_fusion.2 = f32[256,512]{1,0:T(8,128)S(1)} fusion(f32[256,512]{1,0:T(8,128)S(1)} %fusion.45, s32[1024]{0:T(1024)} %bitcast.106, bf16[128,8,512]{2,1,0:T(8,128)(2,1)S(1)} %all-to-all-done.1), kind=kCustom, calls=%fused_computation.28 | custom fusion | flops 1048576 | bytes 1572864 | tf_op jit(solution)/shard_map/scatter-add | solution.py:181
  124.3 1.4 fusion.47
  125.7 0.9 copy-done.10
  127.4 2.1 fusion.16
  129.9 0.5 fusion.33
  130.4 63.1 %psum.47 = f32[4,512]{1,0:T(4,128)S(1)} all-reduce(f32[4,512]{1,0:T(4,128)S(1)} %pad_maximum_fusion.5), channel_id=1, replica_groups=mesh['lat'=4,'lon'=32] {'lat','lon'}, use_global_device_ids=true, to_apply=%region_22.23 | all-reduce | flops 2048 | bytes 16384 | tf_op jit(solution)/shard_map/psum | solution.py:189
  193.5 0.6 broadcast_multiply_fusion.6
  194.1 0.9 fusion.32
  195.0 86.8 %all-reduce.3.cloned.1.call-done = (f32[512,512]{1,0:T(8,128)}, f32[512,512]{1,0:T(8,128)}, f32[512,512]{1,0:T(8,128)}, f32[1024,512]{1,0:T(8,128)}, f32[512,512]{1,0:T(8,128)}) async-done(((f32[512,512]{1,0:T(8,128)}, f32[512,512]{1,0:T(8,128)}, f32[512,512]{1,0:T(8,128)}, f32[1024,512]{1,0:T(8,128)}, f32[512,512]{1,0:T(8,128)}), (f32[512,512]{1,0:T(8,128)}, f32[512,512]{1,0:T(8,128)}, ...) | async-done | bytes 6291472 | tf_op jit(solution)/shard_map/psum | solution.py:189
  281.9 3.3 %broadcast_multiply_fusion = f32[1024,512]{1,0:T(8,128)} fusion(f32[1024,512]{1,0:T(8,128)} %get-tuple-element.42), kind=kLoop, calls=%fused_computation.46 | loop fusion | flops 524288 | bytes 4194304 | tf_op jit(solution)/shard_map/mul | solution.py:207
  285.2 1.6 broadcast_multiply_fusion.1
  286.8 0.7 copy-done.20
  287.5 1.6 broadcast_multiply_fusion.3
  (109 shorter events, 2.7 us)
Async XLA Ops:
  7.2 48.1 %copy-start = (bf16[512,512]{1,0:T(8,128)(2,1)S(1)}, bf16[512,512]{1,0:T(8,128)(2,1)}, u32[]{:S(2)}) copy-start(bf16[512,512]{1,0:T(8,128)(2,1)} %param.26) | copy-start | bytes 1572868
  11.0 26.9 %collective-permute-start = (bf16[128,512]{1,0:T(8,128)(2,1)S(1)}, bf16[128,512]{1,0:T(8,128)(2,1)S(1)}, u32[]{:S(2)}, u32[]{:S(2)}) collective-permute-start(bf16[128,512]{1,0:T(8,128)(2,1)S(1)} %get-tuple-element.48), channel_id=1, source_target_pairs={{0,1},{1,2},{2,3},{3,4},{4,5},{5,6},{6,7},{7,8},{8,9},{9,10},{10,1... | collective-permute-start | bytes 393224 | tf_op jit(solution)/shard_map/ppermute | solution.py:20
  13.7 24.3 %collective-permute-start.1 = (bf16[128,512]{1,0:T(8,128)(2,1)S(1)}, bf16[128,512]{1,0:T(8,128)(2,1)}, u32[]{:S(2)}, u32[]{:S(2)}) collective-permute-start(bf16[128,512]{1,0:T(8,128)(2,1)S(1)} %get-tuple-element.49), channel_id=1, source_target_pairs={{1,0},{2,1},{3,2},{4,3},{5,4},{6,5},{7,6},{8,7},{9,8},{10,9},{11,1... | collective-permute-start | bytes 393224 | tf_op jit(solution)/shard_map/ppermute | solution.py:21
  14.4 0.6 copy-start.35
  15.0 15.8 %copy-start.34 = (s32[4,256]{1,0:T(4,128)S(1)}, s32[4,256]{1,0:T(4,128)}, u32[]{:S(2)}) copy-start(s32[4,256]{1,0:T(4,128)} %param.19) | copy-start | bytes 12292
  15.0 18.5 %copy-start.1 = (bf16[256,512]{1,0:T(8,128)(2,1)S(1)}, bf16[256,512]{1,0:T(8,128)(2,1)}, u32[]{:S(2)}) copy-start(bf16[256,512]{1,0:T(8,128)(2,1)} %param.18) | copy-start | bytes 786436
  15.0 18.5 %copy-start.13 = (bf16[1024,512]{1,0:T(8,128)(2,1)S(1)}, bf16[1024,512]{1,0:T(8,128)(2,1)}, u32[]{:S(2)}) copy-start(bf16[1024,512]{1,0:T(8,128)(2,1)} %param.28) | copy-start | bytes 3145732
  15.0 18.5 %copy-start.33 = (f32[512]{0:T(512)S(1)}, f32[512]{0:T(512)}, u32[]{:S(2)}) copy-start(f32[512]{0:T(512)} %param.22) | copy-start | bytes 6148
  20.1 30.0 %all-to-all-start = ((bf16[128,8,512]{2,1,0:T(8,128)(2,1)}), bf16[128,8,512]{2,1,0:T(8,128)(2,1)S(1)}, u32[]{:S(2)}, u32[]{:S(2)}) async-start(bf16[128,8,512]{2,1,0:T(8,128)(2,1)} %bitcast.3), calls=%async_computation | async-start | bytes 2097152 | tf_op jit(solution)/shard_map/all_to_all | solution.py:146
  38.9 11.2 %copy-start.36 = (s32[1024]{0:T(1024)S(1)}, s32[1024]{0:T(1024)}, u32[]{:S(2)}) copy-start(s32[1024]{0:T(1024)} %pad_clamp_fusion) | copy-start | bytes 12292
  44.0 8.7 %copy-start.5 = (bf16[1024,512]{1,0:T(8,128)(2,1)S(1)}, bf16[1024,512]{1,0:T(8,128)(2,1)}, u32[]{:S(2)}) copy-start(bf16[1024,512]{1,0:T(8,128)(2,1)} %gather_fusion) | copy-start | bytes 3145732
  56.9 0.7 copy-start.37
  57.4 3.9 %copy-start.2 = (f32[1536,512]{1,0:T(8,128)}, f32[1536,512]{1,0:T(8,128)S(1)}, u32[]{:S(2)}) copy-start(f32[1536,512]{1,0:T(8,128)S(1)} %subtract_multiply_fusion) | copy-start | bytes 9437188
  57.4 2.0 copy-start.14
  57.4 2.5 copy-start.29
  57.4 2.5 copy-start.40
  57.4 2.8 copy-start.30
  57.4 2.8 copy-start.41
  59.9 1.8 copy-start.11
  60.2 1.6 copy-start.26
  61.2 10.9 %copy-start.8 = (bf16[256,512]{1,0:T(8,128)(2,1)}, bf16[256,512]{1,0:T(8,128)(2,1)S(1)}, u32[]{:S(2)}) copy-start(bf16[256,512]{1,0:T(8,128)(2,1)S(1)} %get-tuple-element.56) | copy-start | bytes 786436
  61.8 1.8 copy-start.17
  62.8 1.0 copy-start.16
  62.8 1.2 copy-start.24
  82.5 1.9 copy-start.3
  83.4 24.7 %collective-permute-start.2 = (bf16[128,512]{1,0:T(8,128)(2,1)S(1)}, bf16[128,512]{1,0:T(8,128)(2,1)}, u32[]{:S(2)}, u32[]{:S(2)}) collective-permute-start(bf16[128,512]{1,0:T(8,128)(2,1)S(1)} %get-tuple-element.46), channel_id=1, source_target_pairs={{0,1},{1,2},{2,3},{3,4},{4,5},{5,6},{6,7},{7,8},{8,9},{9,10},{10,1... | collective-permute-start | bytes 393224 | tf_op jit(solution)/shard_map/ppermute | solution.py:20
  84.5 23.6 %collective-permute-start.3 = (bf16[128,512]{1,0:T(8,128)(2,1)}, bf16[128,512]{1,0:T(8,128)(2,1)}, u32[]{:S(2)}, u32[]{:S(2)}) collective-permute-start(bf16[128,512]{1,0:T(8,128)(2,1)} %get-tuple-element.47), channel_id=1, source_target_pairs={{1,0},{2,1},{3,2},{4,3},{5,4},{6,5},{7,6},{8,7},{9,8},{10,9},{11,1... | collective-permute-start | bytes 393224 | tf_op jit(solution)/shard_map/ppermute | solution.py:21
  89.0 10.9 %copy-start.6 = (bf16[1024,512]{1,0:T(8,128)(2,1)S(1)}, bf16[1024,512]{1,0:T(8,128)(2,1)}, u32[]{:S(2)}) copy-start(bf16[1024,512]{1,0:T(8,128)(2,1)} %gather_fusion) | copy-start | bytes 3145732
  89.0 27.9 %all-to-all-start.1 = ((bf16[128,8,512]{2,1,0:T(8,128)(2,1)}), bf16[128,8,512]{2,1,0:T(8,128)(2,1)S(1)}, u32[]{:S(2)}, u32[]{:S(2)}) async-start(bf16[128,8,512]{2,1,0:T(8,128)(2,1)} %convert_bitcast_fusion), calls=%async_computation.1 | async-start | bytes 2097152 | tf_op jit(solution)/shard_map/all_to_all | solution.py:178
  97.5 184.4 %all-reduce.3.cloned.1.call-start = ((), (), s32[]{:S(2)}) async-start(), calls=%async_computation.2 | async-start | bytes 12582912 | tf_op jit(solution)/shard_map/psum | solution.py:189
  99.9 5.0 %copy-start.9 = (bf16[256,512]{1,0:T(8,128)(2,1)S(1)}, bf16[256,512]{1,0:T(8,128)(2,1)}, u32[]{:S(2)}) copy-start(bf16[256,512]{1,0:T(8,128)(2,1)} %copy-done.8) | copy-start | bytes 786436
  99.9 5.0 %copy-start.12 = (bf16[256,512]{1,0:T(8,128)(2,1)S(1)}, bf16[256,512]{1,0:T(8,128)(2,1)}, u32[]{:S(2)}) copy-start(bf16[256,512]{1,0:T(8,128)(2,1)} %copy-done.11) | copy-start | bytes 786436
  99.9 5.3 %copy-start.27 = (f32[256,512]{1,0:T(8,128)S(1)}, f32[256,512]{1,0:T(8,128)}, u32[]{:S(2)}) copy-start(f32[256,512]{1,0:T(8,128)} %copy-done.26) | copy-start | bytes 1572868
  99.9 5.3 %copy-start.31 = (bf16[256,512]{1,0:T(8,128)(2,1)S(1)}, bf16[256,512]{1,0:T(8,128)(2,1)}, u32[]{:S(2)}) copy-start(bf16[256,512]{1,0:T(8,128)(2,1)} %param.31) | copy-start | bytes 786436
  104.9 1.7 copy-start.7
  105.2 2.9 copy-start.4
  105.3 2.9 slice-start
  125.7 0.9 copy-start.10
  125.7 1.3 copy-start.15
  125.7 1.6 copy-start.28
  127.0 2.5 copy-start.18
  127.0 2.5 copy-start.23
  127.0 2.8 copy-start.25
  127.4 3.0 %copy-start.38 = (f32[512]{0:T(512)S(1)}, f32[512]{0:T(512)}, u32[]{:S(2)}) copy-start(f32[512]{0:T(512)} %get-tuple-element.55) | copy-start | bytes 6148
  127.4 3.0 %copy-start.39 = (f32[512]{0:T(512)S(1)}, f32[512]{0:T(512)}, u32[]{:S(2)}) copy-start(f32[512]{0:T(512)} %get-tuple-element.32) | copy-start | bytes 6148
  127.4 66.7 %copy-start.32 = (bf16[256,512]{1,0:T(8,128)(2,1)S(1)}, bf16[256,512]{1,0:T(8,128)(2,1)}, u32[]{:S(2)}) copy-start(bf16[256,512]{1,0:T(8,128)(2,1)} %param.31) | copy-start | bytes 786436
  281.9 3.3 %copy-start.21 = (f32[512,512]{1,0:T(8,128)S(1)}, f32[512,512]{1,0:T(8,128)}, u32[]{:S(2)}) copy-start(f32[512,512]{1,0:T(8,128)} %get-tuple-element.41) | copy-start | bytes 3145732
  281.9 3.3 %copy-start.22 = (f32[512,512]{1,0:T(8,128)S(1)}, f32[512,512]{1,0:T(8,128)}, u32[]{:S(2)}) copy-start(f32[512,512]{1,0:T(8,128)} %get-tuple-element.43) | copy-start | bytes 3145732
  285.2 1.6 copy-start.19
  285.2 2.3 copy-start.20
Sparse Core Ops, SparseCore 0:
  125.9 155.9 all-reduce.2
where the time goes:
time: 297 us; the launch traced here: 296 us
  waiting for transfers between devices  99.9 us (34%)
  blocking collectives  63.1 us (21%)
  other arithmetic  39.8 us (13%)
  matrix products  28.4 us (10%)
  local copies, waits for them, and re-layouts  27.4 us (9%)
  starting transfers between devices  22.9 us (8%)
  between operations  14.6 us (5%)
    psum x1, waiting for transfers between devices, per_device(): lax.psum((outer_sum(normed, grad_sent), matrices[1], matrices[0], matrice...  86.8 us
    psum x1, blocking collectives, per_device(): lax.psum((outer_sum(normed, grad_sent), matrices[1], matrices[0], matrice...  63.1 us
    dot_general x6, matrix products, outer_sum(): lax.dot_general(former, latter, (((0,), (0,)), ((), ())), preferred_eleme...  11.9 us
    all_to_all x1, starting transfers between devices, per_device(): lax.all_to_all(packed, ('lat', 'lon'), split_axis=0, concat_axis=0, tiled...  10.6 us
    all_to_all x1, starting transfers between devices, per_device(): lax.all_to_all(bucket.astype(jnp.bfloat16), ('lat', 'lon'), split_axis=0,...  8.43 us
    dot_general x6, matrix products, back_dot(): lax.dot_general(former, latter, (((1,), (1,)), ((), ())), preferred_eleme...  8.21 us
    scatter-add x1, other arithmetic, per_device(): grad_extended = jnp.zeros((row_count + 2 * RIM, feature), jnp.float32).at...  7.73 us
    scatter-add x1, other arithmetic, per_device(): grad_sent = grad_sent.at[send_rows].add(returned).astype(jnp.bfloat16)  7.32 us
  transfers between devices with their start and end apart: 7, of which 3 were waited for; matrix products, arithmetic and copies ran while one was open for 14% of the time, Pallas kernels for 0%

commit v1 on v0

v1 whole, which is shorter than its diff:
```python
import types

import jax
import jax.numpy as jnp
from jax import lax
from jax.experimental import pallas as pl
from jax.experimental.pallas import tpu as pltpu
from jax.sharding import PartitionSpec as P

MESH = pl.DeviceIdType.MESH
EPS = 1e-05
D = 512
ROWS = 256
RIM = 128
DEG = 4
CDEG = 2
EDGES = DEG + CDEG
DEVICES = 128
CAP = 8
SLOTS = DEVICES * CAP
F32 = jnp.float32
BF16 = jnp.bfloat16

NODE_OUT, NODE_SELF, NODE_AGG, RECEIVE, EDGE, SEND = range(6)


def mm(a, b):
    return jnp.dot(a, b, preferred_element_type=F32)


def mm_bt(a, b):
    return lax.dot_general(a, b, (((1,), (1,)), ((), ())), preferred_element_type=F32)


def mm_at(a, b):
    return lax.dot_general(a, b, (((0,), (0,)), ((), ())), preferred_element_type=F32)


def mean_row(v):
    return jnp.mean(v, axis=-1, keepdims=True)


def silu_parts(v):
    gate = 0.5 * jnp.tanh(0.5 * v) + 0.5
    out = v * gate
    return out, gate + out * (1.0 - gate)


def norm_rows(v):
    centred = v - mean_row(v)
    inverse = lax.rsqrt(mean_row(centred * centred) + EPS)
    return centred * inverse, inverse


def col_sum(v):
    return jnp.sum(v, axis=0, keepdims=True)


def lane_hot(column, width):
    lanes = lax.broadcasted_iota(jnp.int32, (column.shape[0], width), 1)
    return jnp.where(lanes == column, 1.0, 0.0).astype(BF16)


def sub_hot(row, height):
    subs = lax.broadcasted_iota(jnp.int32, (height, row.shape[1]), 0)
    return jnp.where(subs == row, 1.0, 0.0).astype(BF16)


def to_pairs(rows):
    k = rows.shape[0] // CAP
    left = rows[:, : D // 2].reshape(k, CAP, D // 2)
    right = rows[:, D // 2 :].reshape(k, CAP, D // 2)
    return jnp.concatenate([left, right], axis=1).astype(BF16)


def from_pairs(pairs):
    k = pairs.shape[0]
    wide = pairs.astype(F32)
    left = wide[:, :CAP].reshape(k * CAP, D // 2)
    right = wide[:, CAP:].reshape(k * CAP, D // 2)
    return jnp.concatenate([left, right], axis=1).astype(BF16)


INPUTS = ["lat", "near", "slot", "csend", "ngain", "sw", "rw", "ebias", "ew", "egain", "ni", "nbias", "no", "cot"]
OUTPUTS = ["newlat", "glat", "res", "vout"]


def scratch():
    dma = pltpu.SemaphoreType.DMA
    half = (DEVICES, 2 * CAP, D // 2)
    return {
        "ext_n": pltpu.VMEM((ROWS + 2 * RIM, D), BF16),
        "lhat": pltpu.VMEM((ROWS, D), F32),
        "linv": pltpu.VMEM((ROWS, 1), F32),
        "pk": pltpu.VMEM(half, BF16),
        "arr": pltpu.VMEM(half, BF16),
        "pk2": pltpu.VMEM(half, BF16),
        "arr2": pltpu.VMEM(half, BF16),
        "arr_n": pltpu.VMEM((SLOTS, D), BF16),
        "cols": pltpu.VMEM((EDGES, ROWS, 1), jnp.int32),
        "recv": pltpu.VMEM((ROWS, D), F32),
        "gh": pltpu.VMEM((ROWS, D), F32),
        "npre": pltpu.VMEM((ROWS, D), F32),
        "sent_ext": pltpu.VMEM((ROWS + 2 * RIM, D), BF16),
        "act": pltpu.VMEM((EDGES, ROWS, D), BF16),
        "slope": pltpu.VMEM((EDGES, ROWS, D), F32),
        "hat": pltpu.VMEM((EDGES, ROWS, D), F32),
        "einv": pltpu.VMEM((EDGES, ROWS, 1), F32),
        "hsum": pltpu.VMEM((ROWS, D), F32),
        "cn": pltpu.VMEM((CDEG, ROWS, D), BF16),
        "geb": pltpu.VMEM((EDGES, ROWS, D), BF16),
        "gext": pltpu.VMEM((ROWS + 2 * RIM, D), F32),
        "rims": pltpu.VMEM((4, RIM, D), BF16),
        "gnp": pltpu.VMEM((ROWS, D), BF16),
        "aggr": pltpu.VMEM((ROWS, D), BF16),
        "grecv": pltpu.VMEM((ROWS, D), BF16),
        "gnb": pltpu.VMEM((ROWS, D), F32),
        "acc": pltpu.VMEM((D, D), F32),
        "part": pltpu.VMEM((6, D, D), BF16),
        "crecv": pltpu.VMEM((3, D, D), BF16),
        "s1": pltpu.VMEM((3, D, D), BF16),
        "r1": pltpu.VMEM((3, 3, D // 4, D), BF16),
        "s2": pltpu.VMEM((3, D // 4, D), BF16),
        "r2": pltpu.VMEM((3, 3, D // 16, D), BF16),
        "s3": pltpu.VMEM((3, D // 16, D), BF16),
        "r3": pltpu.VMEM((3, 3, D // 16, D // 4), BF16),
        "vec": pltpu.VMEM((4, 8, D), F32),
        "vrecv": pltpu.VMEM((4, 4, 8, D), F32),
        "hs": dma((2,)), "hr": dma((2,)), "hs2": dma((2,)), "hr2": dma((2,)),
        "as_": dma, "ar": dma, "as2": dma, "ar2": dma,
        "cs": dma((3,)), "cr": dma((3,)), "gcs": dma((3,)), "gcr": dma((3,)),
        "s1s": dma((3, 3)), "s1r": dma((3, 3)), "s2s": dma((3, 3)), "s2r": dma((3, 3)),
        "s3s": dma((3, 3)), "s3r": dma((3, 3)), "g1s": dma((3, 3)), "g1r": dma((3, 3)),
        "g2s": dma((3, 3)), "g2r": dma((3, 3)), "g3s": dma((3, 3)), "g3r": dma((3, 3)),
        "vs": dma((4, 3)), "vr": dma((4, 3)),
    }


def body(*refs):
    r = types.SimpleNamespace(**dict(zip(INPUTS + OUTPUTS + list(scratch()), refs)))
    la = lax.axis_index("lat")
    lo = lax.axis_index("lon")
    me = la * 32 + lo
    z, y, x, c = la, lo // 8, lax.rem(lo // 2, 4), lax.rem(lo, 2)

    def dev(t):
        return (t // 32, lax.rem(t, 32))

    def at(z, y, x, c):
        return (z, y * 8 + x * 2 + c)

    coord = {"x": x, "y": y, "z": z}

    def peer(axis, d):
        p = dict(coord)
        p[axis] = lax.rem(coord[axis] + d, 4)
        return at(p["z"], p["y"], p["x"], c), p[axis]

    def rcopy(src, dst, ssem, rsem, device):
        return pltpu.make_async_remote_copy(src, dst, ssem, rsem, device_id=device, device_id_type=MESH)

    bar = pltpu.get_barrier_semaphore()

    @pl.loop(1, DEVICES)
    def _(k):
        pl.semaphore_signal(bar, inc=1, device_id=dev(lax.rem(me + k, DEVICES)), device_id_type=MESH)

    h, inv = norm_rows(r.lat[...].astype(F32))
    r.lhat[...] = h
    r.linv[...] = inv
    r.ext_n[RIM : RIM + ROWS] = (h * r.ngain[...]).astype(BF16)

    idx = jnp.concatenate([r.near[...], r.slot[...], jnp.zeros((2, ROWS), jnp.int32)], axis=0)
    idx_t = jnp.transpose(idx)
    for k in range(EDGES):
        r.cols[k] = idx_t[:, k : k + 1]
    send_t = jnp.transpose(r.csend[...].reshape(8, 128))
    for j in range(8):
        rows = mm(lane_hot(send_t[:, j : j + 1], ROWS), r.ext_n[RIM : RIM + ROWS])
        r.pk[16 * j : 16 * j + 16] = to_pairs(rows)

    pl.semaphore_wait(bar, DEVICES - 1)

    west = (la, lax.rem(lo + 31, 32))
    east = (la, lax.rem(lo + 1, 32))
    halo = [
        rcopy(r.ext_n.at[pl.ds(2 * RIM, RIM)], r.ext_n.at[pl.ds(0, RIM)], r.hs.at[0], r.hr.at[0], east),
        rcopy(r.ext_n.at[pl.ds(RIM, RIM)], r.ext_n.at[pl.ds(3 * RIM, RIM)], r.hs.at[1], r.hr.at[1], west),
    ]
    for q in halo:
        q.start()

    @pl.loop(1, DEVICES)
    def _(k):
        t = lax.rem(me + k, DEVICES)
        rcopy(r.pk.at[t], r.arr.at[me], r.as_, r.ar, dev(t)).start()

    r.arr[me] = r.pk[me]

    def own():
        return r.ext_n[RIM : RIM + ROWS]

    r.recv[...] = mm(own(), r.rw[...]) + r.ebias[...]
    r.sent_ext[RIM : RIM + ROWS] = mm(own(), r.sw[...]).astype(BF16)
    r.gh[...] = mm_bt(r.cot[...], r.no[...])
    r.npre[...] = mm(own(), r.ni[0:D]) + r.nbias[...]
    r.hsum[...] = jnp.zeros((ROWS, D), F32)
    for q in halo:
        q.wait()
    r.sent_ext[0:RIM] = mm(r.ext_n[0:RIM], r.sw[...]).astype(BF16)
    r.sent_ext[3 * RIM : 4 * RIM] = mm(r.ext_n[3 * RIM : 4 * RIM], r.sw[...]).astype(BF16)

    def edge_forward(k, senders):
        a, s = silu_parts(senders + r.recv[...])
        a = a.astype(BF16)
        r.act[k] = a
        r.slope[k] = s
        h, inv = norm_rows(mm(a, r.ew[...]))
        r.hat[k] = h
        r.einv[k] = inv
        r.hsum[...] += h

    @pl.loop(0, DEG)
    def _(k):
        edge_forward(k, mm(lane_hot(r.cols[k], ROWS + 2 * RIM), r.sent_ext[...]))

    everything = rcopy(r.pk.at[pl.ds(0, DEVICES - 1)], r.arr.at[pl.ds(0, DEVICES - 1)], r.as_, r.ar, west)
    everything.wait()

    @pl.loop(0, 8)
    def _(j):
        r.arr_n[pl.ds(pl.multiple_of(j * 128, 128), 128)] = from_pairs(r.arr[pl.ds(j * 16, 16)])

    @pl.loop(0, CDEG)
    def _(k):
        rows = mm(lane_hot(r.cols[DEG + k], SLOTS), r.arr_n[...]).astype(BF16)
        r.cn[k] = rows
        edge_forward(DEG + k, mm(rows, r.sw[...]).astype(BF16).astype(F32))

    aggregate = (r.hsum[...] * r.egain[...]).astype(BF16)
    hidden, node_slope = silu_parts(r.npre[...] + mm(aggregate, r.ni[D : 2 * D]))
    hidden = hidden.astype(BF16)
    r.newlat[...] = (r.lat[...].astype(F32) + mm(hidden, r.no[...])).astype(BF16)
    gnp = (r.gh[...] * node_slope).astype(BF16)
    r.gnp[...] = gnp
    r.aggr[...] = aggregate
    gagg = mm_bt(gnp, r.ni[D : 2 * D])
    r.vec[0] = jnp.zeros((8, D), F32)
    r.vec[0, 2:3] = col_sum(gagg * r.hsum[...])
    r.vec[0, 3:4] = col_sum(gnp.astype(F32))
    r.part[NODE_OUT] = mm_at(hidden, r.cot[...]).astype(BF16)
    r.part[NODE_SELF] = mm_at(own(), r.gnp[...]).astype(BF16)

    def core_copy(p):
        return rcopy(r.part.at[2 * p + 1 - c], r.crecv.at[p], r.cs.at[p], r.cr.at[p], at(z, y, x, 1 - c))

    core_copy(0).start()
    r.part[NODE_AGG] = mm_at(r.aggr[...], r.gnp[...]).astype(BF16)

    up = gagg * r.egain[...]
    r.npre[...] = up - mean_row(up)
    r.gh[...] = up
    r.recv[...] = jnp.zeros((ROWS, D), F32)
    r.acc[...] = jnp.zeros((D, D), F32)

    def edge_backward(k):
        h = r.hat[k]
        g = (r.einv[k] * (r.npre[...] - h * mean_row(r.gh[...] * h))).astype(BF16)
        ge = mm_bt(g, r.ew[...]) * r.slope[k]
        r.recv[...] += ge
        r.geb[k] = ge.astype(BF16)
        r.acc[...] += mm_at(r.act[k], g)

    pl.loop(DEG, EDGES)(edge_backward)

    for j in range(4):
        block = jnp.zeros((256, D), F32)
        for k in range(CDEG):
            block += mm(sub_hot(r.slot[k : k + 1, :] - 256 * j, 256), r.geb[DEG + k])
        r.pk2[32 * j : 32 * j + 32] = to_pairs(block)

    @pl.loop(1, DEVICES)
    def _(k):
        t = lax.rem(me + k, DEVICES)
        rcopy(r.pk2.at[t], r.arr2.at[me], r.as2, r.ar2, dev(t)).start()

    r.arr2[me] = r.pk2[me]

    pl.loop(0, DEG)(edge_backward)
    r.part[EDGE] = r.acc[...].astype(BF16)
    for j in range(4):
        block = jnp.zeros((RIM, D), F32)
        for k in range(DEG):
            block += mm(sub_hot(r.near[k : k + 1, :] - RIM * j, RIM), r.geb[k])
        r.gext[RIM * j : RIM * j + RIM] = block
    r.rims[0] = r.gext[0:RIM].astype(BF16)
    r.rims[1] = r.gext[3 * RIM : 4 * RIM].astype(BF16)
    halo_back = [
        rcopy(r.rims.at[1], r.rims.at[2], r.hs2.at[0], r.hr2.at[0], east),
        rcopy(r.rims.at[0], r.rims.at[3], r.hs2.at[1], r.hr2.at[1], west),
    ]
    for q in halo_back:
        q.start()
    r.vec[0, 1:2] = col_sum(r.recv[...])
    r.grecv[...] = r.recv[...].astype(BF16)
    r.part[RECEIVE] = mm_at(own(), r.grecv[...]).astype(BF16)
    r.acc[...] = mm_at(r.ext_n[...], r.gext[...].astype(BF16))
    for k in range(CDEG):
        r.acc[...] += mm_at(r.cn[k], r.geb[DEG + k])
    r.part[SEND] = r.acc[...].astype(BF16)
    core_copy(1).start()
    core_copy(2).start()
    local_back = mm_bt(r.gnp[...], r.ni[0:D]) + mm_bt(r.grecv[...], r.rw[...])
    r.gnb[...] = local_back
    through_sent = jnp.sum(r.sw[...].astype(F32) * r.acc[...], axis=1, keepdims=True)
    through_sent = jnp.transpose(jnp.broadcast_to(through_sent, (D, 128)))[0:1]
    r.vec[0, 0:1] = col_sum(r.lhat[...] * local_back) + through_sent / r.ngain[...]

    orders = ("xyz", "yzx", "zxy")
    scale = float(ROWS * DEVICES) ** -0.5

    def rs1(p, d):
        device, pos = peer(orders[p][0], d)
        return rcopy(r.s1.at[p, pl.ds(pl.multiple_of(pos * 128, 128), 128)], r.r1.at[p, d - 1], r.s1s.at[p, d - 1], r.s1r.at[p, d - 1], device)

    def rs2(p, d):
        device, pos = peer(orders[p][1], d)
        return rcopy(r.s2.at[p, pl.ds(pl.multiple_of(pos * 32, 32), 32)], r.r2.at[p, d - 1], r.s2s.at[p, d - 1], r.s2r.at[p, d - 1], device)

    def rs3(p, d):
        device, pos = peer(orders[p][2], d)
        return rcopy(r.s3.at[p, :, pl.ds(pl.multiple_of(pos * 128, 128), 128)], r.r3.at[p, d - 1], r.s3s.at[p, d - 1], r.s3r.at[p, d - 1], device)

    def spot(p, level):
        a, b, e = (coord[axis] for axis in orders[p])
        rows, lanes = a * 128 + b * 32, pl.ds(pl.multiple_of(e * 128, 128), 128)
        if level == 3:
            return r.res.at[2 * p + c, pl.ds(pl.multiple_of(rows, 32), 32), lanes]
        if level == 2:
            return r.res.at[2 * p + c, pl.ds(pl.multiple_of(rows, 32), 32)]
        if level == 1:
            return r.res.at[2 * p + c, pl.ds(pl.multiple_of(a * 128, 128), 128)]
        return r.res.at[2 * p + c]

    def ag(p, level, d):
        ssem, rsem = {3: (r.g3s, r.g3r), 2: (r.g2s, r.g2r), 1: (r.g1s, r.g1r)}[level]
        device, _ = peer(orders[p][level - 1], d)
        return rcopy(spot(p, level), spot(p, level), ssem.at[p, d - 1], rsem.at[p, d - 1], device)

    def ag_core(p):
        return rcopy(spot(p, 0), spot(p, 0), r.gcs.at[p], r.gcr.at[p], at(z, y, x, 1 - c))

    def vec_core():
        return rcopy(r.vec.at[0], r.vrecv.at[0, 1], r.vs.at[0, 0], r.vr.at[0, 0], at(z, y, x, 1 - c))

    def vec_ring(level, d):
        axis = "xyz"[level - 1]
        device, _ = peer(axis, d)
        return rcopy(r.vec.at[level], r.vrecv.at[level, d], r.vs.at[level, d - 1], r.vr.at[level, d - 1], device)

    def vec_sum(level):
        axis = "xyz"[level - 1]
        mine = coord[axis]
        r.vrecv[level, 0] = r.vec[level]
        total = jnp.zeros((8, D), F32)
        for i in range(4):
            total += r.vrecv[level, lax.rem(mine - i + 4, 4)]
        return total

    def vec_total(level):
        if level == 0:
            return r.vec[0] + r.vrecv[0, 1]
        return vec_sum(level)

    vec_core().start()

    def fold_core(p):
        core_copy(p).wait()

        @pl.loop(0, 4)
        def _(j):
            rows = pl.ds(pl.multiple_of(j * 128, 128), 128)
            r.s1[p, rows] = (r.part[2 * p + c, rows].astype(F32) + r.crecv[p, rows].astype(F32)).astype(BF16)

        for d in (2, 1, 3):
            rs1(p, d).start()

    def fold1(p):
        total = r.s1[p, pl.ds(pl.multiple_of(coord[orders[p][0]] * 128, 128), 128)].astype(F32)
        for d in (1, 3, 2):
            rs1(p, d).wait()
            total += r.r1[p, d - 1].astype(F32)
        r.s2[p] = total.astype(BF16)
        for d in (2, 1, 3):
            rs2(p, d).start()

    def fold2(p):
        total = r.s2[p, pl.ds(pl.multiple_of(coord[orders[p][1]] * 32, 32), 32)].astype(F32)
        for d in (1, 3, 2):
            rs2(p, d).wait()
            total += r.r2[p, d - 1].astype(F32)
        r.s3[p] = total.astype(BF16)
        for d in (2, 1, 3):
            rs3(p, d).start()

    def fold3(p):
        total = r.s3[p, :, pl.ds(pl.multiple_of(coord[orders[p][2]] * 128, 128), 128)].astype(F32)
        for d in (1, 3, 2):
            rs3(p, d).wait()
            total += r.r3[p, d - 1].astype(F32)
        spot(p, 3)[...] = (total * scale).astype(BF16)
        for d in (2, 1, 3):
            ag(p, 3, d).start()

    def spread(p, level):
        for d in (1, 3, 2):
            ag(p, level, d).wait()
        if level > 1:
            for d in (2, 1, 3):
                ag(p, level - 1, d).start()
        else:
            ag_core(p).start()

    def vec_step(level):
        if level == 0:
            vec_core().wait()
        else:
            for d in (1, 2, 3):
                vec_ring(level, d).wait()
        total = vec_total(level)
        if level < 3:
            r.vec[level + 1] = total
            for d in (1, 2, 3):
                vec_ring(level + 1, d).start()
        else:
            r.vout[...] = total[0:4] * scale

    for p in range(3):
        fold_core(p)
    vec_step(0)
    for p in range(3):
        fold1(p)
    vec_step(1)
    for p in range(3):
        fold2(p)
    vec_step(2)
    for p in range(3):
        fold3(p)
    vec_step(3)

    for q in halo_back:
        q.wait()
    grad_sent = r.gext[RIM : RIM + ROWS] + r.rims[2:4].reshape(ROWS, D).astype(F32)
    rcopy(r.pk2.at[pl.ds(0, DEVICES - 1)], r.arr2.at[pl.ds(0, DEVICES - 1)], r.as2, r.ar2, west).wait()

    @pl.loop(0, 8)
    def _(j):
        r.arr_n[pl.ds(pl.multiple_of(j * 128, 128), 128)] = from_pairs(r.arr2[pl.ds(j * 16, 16)])

    grad_sent += mm(sub_hot(r.csend[...], ROWS), r.arr_n[...])
    up = (r.gnb[...] + mm_bt(grad_sent.astype(BF16), r.sw[...])) * r.ngain[...]
    h = r.lhat[...]
    back = r.linv[...] * (up - mean_row(up) - h * mean_row(up * h))
    r.glat[...] = (r.cot[...].astype(F32) + back).astype(BF16)

    for level in (3, 2, 1):
        for p in range(3):
            spread(p, level)
    for p in range(3):
        ag_core(p).wait()


def per_device(
    latents, near_index, coarse_slot, coarse_send, norm_gain, send_weight, receive_weight, edge_bias,
    edge_weight, edge_gain, node_input, node_bias, node_output, cotangent,
):
    whole = pl.BlockSpec(memory_space=pltpu.VMEM)
    new_latents, grad_latents, sums, vectors = pl.pallas_call(
        body,
        out_shape=(
            jax.ShapeDtypeStruct((ROWS, D), BF16),
            jax.ShapeDtypeStruct((ROWS, D), BF16),
            jax.ShapeDtypeStruct((6, D, D), BF16),
            jax.ShapeDtypeStruct((4, D), F32),
        ),
        in_specs=[whole] * 14,
        out_specs=(whole,) * 4,
        scratch_shapes=list(scratch().values()),
        compiler_params=pltpu.CompilerParams(
            collective_id=0, has_side_effects=True, vmem_limit_bytes=58 * 2**20
        ),
    )(
        latents, near_index, coarse_slot, coarse_send, norm_gain.reshape(1, D), send_weight, receive_weight,
        edge_bias.reshape(1, D), edge_weight, edge_gain.reshape(1, D), node_input, node_bias.reshape(1, D),
        node_output, cotangent,
    )
    wide = sums.astype(F32)
    return (
        new_latents, grad_latents, wide[SEND], wide[RECEIVE], wide[EDGE],
        wide[NODE_SELF : NODE_AGG + 1].reshape(2 * D, D), wide[NODE_OUT], vectors,
    )


def solution(mesh):
    rows, whole = P(("lat", "lon"), None), P()
    split = P(None, ("lat", "lon"))
    return jax.shard_map(
        per_device,
        mesh=mesh,
        in_specs=(rows, split, split, rows) + (whole,) * 9 + (rows,),
        out_specs=(rows, rows) + (whole,) * 6,
        check_vma=False,
    )
```

time: 297 us -> 95.5 us (0.32)
  waiting for transfers between devices: 99.9 us -> 0 us
  Pallas kernels: 0 us -> 86.8 us
  blocking collectives: 63.1 us -> 0 us
  other arithmetic: 39.8 us -> 0.86 us
  matrix products: 28.4 us -> 0 us
  starting transfers between devices: 22.9 us -> 0 us
  local copies, waits for them, and re-layouts: 27.4 us -> 7.08 us
  between operations: 14.6 us -> 0.69 us
    psum x1 -> x0, waiting for transfers between devices: 86.8 us -> none  [per_device(): lax.psum((outer_sum(normed, grad_sent), matrices[1], matrices[0], matrice...]
    pallas_call x0 -> x1, Pallas kernels: none -> 86.8 us  [per_device(): pl.pallas_call(body, out_shape=(jax.ShapeDtypeStruct((ROWS, D), BF16), ja...]
    psum x1 -> x0, blocking collectives: 63.1 us -> none  [per_device(): lax.psum((outer_sum(normed, grad_sent), matrices[1], matrices[0], matrice...]
    dot_general x18 -> x0, matrix products: 28.4 us -> none  [the longest x6 11.9 us: outer_sum(): lax.dot_general(former, latter, (((0,), (0,)), ((), ())), preferred_eleme...]
    all_to_all x2 -> x0, starting transfers between devices: 19.1 us -> none  [the longest x1 10.6 us: per_device(): lax.all_to_all(packed, ('lat', 'lon'), split_axis=0, concat_axis=0, tiled...]
    scatter-add x4 -> x0, other arithmetic: 16.9 us -> none  [the longest x1 7.73 us: per_device(): grad_extended = jnp.zeros((row_count + 2 * RIM, feature), jnp.float32).at...]
    all_to_all x2 -> x0, waiting for transfers between devices: 13 us -> none  [the longest x1 6.91 us: per_device(): lax.all_to_all(bucket.astype(jnp.bfloat16), ('lat', 'lon'), split_axis=0,...]
    gather x3 -> x0, local copies, waits for them, and re-layouts: 12.8 us -> none  [the longest x1 5.08 us: per_device(): extended[near_index]]
  transfers between devices with their start and end apart: 7 -> 0, of which waited for: 3 -> 0; matrix products, arithmetic and copies ran while one was open for 14% -> 0% of each run, Pallas kernels for 0% -> 0%
where the time goes in v1:
time: 95.5 us; the launch traced here: 95.4 us
  Pallas kernels  86.8 us (91%)
  local copies, waits for them, and re-layouts  7.08 us (7%)
    pallas_call x1, Pallas kernels, per_device(): pl.pallas_call(body, out_shape=(jax.ShapeDtypeStruct((ROWS, D), BF16), ja...  86.8 us
    slice x1, local copies, waits for them, and re-layouts, per_device(): wide[NODE_SELF:NODE_AGG + 1].reshape(2 * D, D)  2.99 us
    squeeze x1, local copies, waits for them, and re-layouts, per_device(): wide[NODE_OUT]  2.08 us
    unnamed x11, local copies, waits for them, and re-layouts  2.02 us

profile of v1, /device:TPU:1, one launch (start us, length us, event | category | flops | bytes accessed | tf_op | source)
XLA Modules:
  0.0 95.4 jit_solution(7031346575061394371)
XLA Ops:
  0.6 86.8 %shard_map.197 = (bf16[256,512]{1,0:T(8,128)(2,1)}, bf16[256,512]{1,0:T(8,128)(2,1)}, bf16[6,512,512]{2,1,0:T(8,128)(2,1)}, f32[4,512]{1,0:T(4,128)}) custom-call(bf16[256,512]{1,0:T(8,128)(2,1)} %refs_0_.1, s32[4,256]{1,0:T(4,128)} %refs_1_.1, s32[2,256]{1,0:T(2,128)} %refs_2_.1, s32[1,1024]{1,0:T(1,128)} %refs_3_.1, f32[1,512]{1,0:T(1,128)} %bitcast.14, ...), custom_call_target="tpu_custom_call" | custom-call | tf_op jit(solution)/shard_map/pallas_call | solution.py:478
  87.4 0.0 copy-start
  87.4 3.0 %slice.23 = f32[2,512,512]{2,1,0:T(8,128)} slice(bf16[6,512,512]{2,1,0:T(8,128)(2,1)} %get-tuple-element.14), slice={[1:3], [0:512], [0:512]} | slice | bytes 4194304 | tf_op jit(solution)/shard_map/slice | solution.py:500
  90.4 0.0 copy-done
  90.4 0.9 convert_element_type.3
  91.3 0.0 copy-start.2
  91.3 0.0 copy-start.1
  91.3 0.0 copy-start.3
  91.3 2.1 %slice_bitcast_fusion = (f32[512,512]{1,0:T(8,128)}, f32[512,512]{1,0:T(8,128)}, f32[512,512]{1,0:T(8,128)}, f32[512,512]{1,0:T(8,128)}) fusion(f32[6,512,512]{2,1,0:T(8,128)S(1)} %convert_element_type.3), kind=kLoop, calls=%fused_computation | loop fusion | bytes 8388608 | tf_op jit(solution)/shard_map/squeeze | solution.py:500
  93.4 0.0 copy-done.2
  93.4 0.7 copy.25
  94.1 0.0 copy-done.1
  94.1 0.7 copy.26
  94.8 0.0 copy-done.3
  94.8 0.6 copy.27
Async XLA Ops:
  87.4 3.0 %copy-start = (bf16[6,512,512]{2,1,0:T(8,128)(2,1)S(1)}, bf16[6,512,512]{2,1,0:T(8,128)(2,1)}, u32[]{:S(2)}) copy-start(bf16[6,512,512]{2,1,0:T(8,128)(2,1)} %get-tuple-element.14) | copy-start | bytes 9437188
  91.3 2.1 %copy-start.2 = (bf16[256,512]{1,0:T(8,128)(2,1)S(1)}, bf16[256,512]{1,0:T(8,128)(2,1)}, u32[]{:S(2)}) copy-start(bf16[256,512]{1,0:T(8,128)(2,1)} %get-tuple-element.28) | copy-start | bytes 786436
  91.3 2.8 %copy-start.1 = (bf16[256,512]{1,0:T(8,128)(2,1)S(1)}, bf16[256,512]{1,0:T(8,128)(2,1)}, u32[]{:S(2)}) copy-start(bf16[256,512]{1,0:T(8,128)(2,1)} %get-tuple-element.29) | copy-start | bytes 786436
  91.3 3.5 %copy-start.3 = (f32[4,512]{1,0:T(4,128)S(1)}, f32[4,512]{1,0:T(4,128)}, u32[]{:S(2)}) copy-start(f32[4,512]{1,0:T(4,128)} %get-tuple-element.35) | copy-start | bytes 24580

commit v2 on v1

--- a/solution.py
+++ b/solution.py
@@ -22,6 +22,22 @@
 BF16 = jnp.bfloat16
 
 NODE_OUT, NODE_SELF, NODE_AGG, RECEIVE, EDGE, SEND = range(6)
+
+
+def exchange_order():
+    cube = [(i, j, k) for i in range(4) for j in range(4) for k in range(4)]
+    cube.sort(key=lambda d: (-sum(min(v, 4 - v) for v in d), [-v for v in d]))
+    order = []
+    for d in cube:
+        for sign in (1, -1):
+            for turn in range(3):
+                e = tuple((sign * v) % 4 for v in d[turn:] + d[:turn])
+                if e not in order:
+                    order.append(e)
+    return [e + (core,) for e in order for core in (0, 1) if any(e) or core]
+
+
+ORDER = exchange_order()
 
 
 def mm(a, b):
@@ -117,21 +133,20 @@
         "gnb": pltpu.VMEM((ROWS, D), F32),
         "acc": pltpu.VMEM((D, D), F32),
         "part": pltpu.VMEM((6, D, D), BF16),
-        "crecv": pltpu.VMEM((3, D, D), BF16),
-        "s1": pltpu.VMEM((3, D, D), BF16),
-        "r1": pltpu.VMEM((3, 3, D // 4, D), BF16),
-        "s2": pltpu.VMEM((3, D // 4, D), BF16),
-        "r2": pltpu.VMEM((3, 3, D // 16, D), BF16),
-        "s3": pltpu.VMEM((3, D // 16, D), BF16),
-        "r3": pltpu.VMEM((3, 3, D // 16, D // 4), BF16),
+        "crecv": pltpu.VMEM((6, D // 2, D), BF16),
+        "s1": pltpu.VMEM((6, D // 2, D), BF16),
+        "r1": pltpu.VMEM((6, 3, D // 8, D), BF16),
+        "s2": pltpu.VMEM((6, D // 8, D), BF16),
+        "r2": pltpu.VMEM((6, 3, D // 32, D), BF16),
+        "r3": pltpu.VMEM((6, 4, D // 32, D), BF16),
         "vec": pltpu.VMEM((4, 8, D), F32),
         "vrecv": pltpu.VMEM((4, 4, 8, D), F32),
         "hs": dma((2,)), "hr": dma((2,)), "hs2": dma((2,)), "hr2": dma((2,)),
         "as_": dma, "ar": dma, "as2": dma, "ar2": dma,
-        "cs": dma((3,)), "cr": dma((3,)), "gcs": dma((3,)), "gcr": dma((3,)),
-        "s1s": dma((3, 3)), "s1r": dma((3, 3)), "s2s": dma((3, 3)), "s2r": dma((3, 3)),
-        "s3s": dma((3, 3)), "s3r": dma((3, 3)), "g1s": dma((3, 3)), "g1r": dma((3, 3)),
-        "g2s": dma((3, 3)), "g2r": dma((3, 3)), "g3s": dma((3, 3)), "g3r": dma((3, 3)),
+        "cs": dma((6,)), "cr": dma((6,)), "gcs": dma((6,)), "gcr": dma((6,)),
+        "s1s": dma((6, 3)), "s1r": dma((6, 3)), "s2s": dma((6, 3)), "s2r": dma((6, 3)),
+        "s3s": dma((6, 3)), "s3r": dma((6, 3)), "g1s": dma((6, 3)), "g1r": dma((6, 3)),
+        "g2s": dma((6, 3)), "g2r": dma((6, 3)),
         "vs": dma((4, 3)), "vr": dma((4, 3)),
     }
 
@@ -143,9 +158,6 @@
     me = la * 32 + lo
     z, y, x, c = la, lo // 8, lax.rem(lo // 2, 4), lax.rem(lo, 2)
 
-    def dev(t):
-        return (t // 32, lax.rem(t, 32))
-
     def at(z, y, x, c):
         return (z, y * 8 + x * 2 + c)
 
@@ -159,11 +171,126 @@
     def rcopy(src, dst, ssem, rsem, device):
         return pltpu.make_async_remote_copy(src, dst, ssem, rsem, device_id=device, device_id_type=MESH)
 
+    orders = {m: ("xyz", "yzx", "zxy")[m % 3] for m in range(6)}
+    scale = float(ROWS * DEVICES) ** -0.5
+    other = at(z, y, x, 1 - c)
+
+    def half(core):
+        return pl.ds(pl.multiple_of(core * 256, 256), 256)
+
+    def core_copy(m):
+        return rcopy(r.part.at[m, half(1 - c)], r.crecv.at[m], r.cs.at[m], r.cr.at[m], other)
+
+    def rs1(m, d):
+        device, pos = peer(orders[m][0], d)
+        rows = pl.ds(pl.multiple_of(pos * 64, 64), 64)
+        return rcopy(r.s1.at[m, rows], r.r1.at[m, d - 1], r.s1s.at[m, d - 1], r.s1r.at[m, d - 1], device)
+
+    def rs2(m, d):
+        device, pos = peer(orders[m][1], d)
+        rows = pl.ds(pl.multiple_of(pos * 16, 16), 16)
+        return rcopy(r.s2.at[m, rows], r.r2.at[m, d - 1], r.s2s.at[m, d - 1], r.s2r.at[m, d - 1], device)
+
+    def swap3(m, d):
+        device, _ = peer(orders[m][2], d)
+        return rcopy(r.r3.at[m, 0], r.r3.at[m, d], r.s3s.at[m, d - 1], r.s3r.at[m, d - 1], device)
+
+    def spot(m, level):
+        a, b = coord[orders[m][0]] * 64, coord[orders[m][1]] * 16
+        if level == 2:
+            return r.res.at[m, pl.ds(pl.multiple_of(c * 256 + a + b, 16), 16)]
+        if level == 1:
+            return r.res.at[m, pl.ds(pl.multiple_of(c * 256 + a, 64), 64)]
+        return r.res.at[m, half(c)]
+
+    def ag(m, level, d):
+        ssem, rsem = {2: (r.g2s, r.g2r), 1: (r.g1s, r.g1r)}[level]
+        device, _ = peer(orders[m][level - 1], d)
+        return rcopy(spot(m, level), spot(m, level), ssem.at[m, d - 1], rsem.at[m, d - 1], device)
+
+    def ag_core(m):
+        return rcopy(spot(m, 0), spot(m, 0), r.gcs.at[m], r.gcr.at[m], other)
+
+    def fold_core(m):
+        core_copy(m).wait()
+        r.s1[m] = (r.part[m, half(c)].astype(F32) + r.crecv[m].astype(F32)).astype(BF16)
+        for d in (2, 1, 3):
+            rs1(m, d).start()
+
+    def fold1(m):
+        total = r.s1[m, pl.ds(pl.multiple_of(coord[orders[m][0]] * 64, 64), 64)].astype(F32)
+        for d in (1, 3, 2):
+            rs1(m, d).wait()
+            total += r.r1[m, d - 1].astype(F32)
+        r.s2[m] = total.astype(BF16)
+        for d in (2, 1, 3):
+            rs2(m, d).start()
+
+    def fold2(m):
+        total = r.s2[m, pl.ds(pl.multiple_of(coord[orders[m][1]] * 16, 16), 16)].astype(F32)
+        for d in (1, 3, 2):
+            rs2(m, d).wait()
+            total += r.r2[m, d - 1].astype(F32)
+        r.r3[m, 0] = total.astype(BF16)
+        for d in (2, 1, 3):
+            swap3(m, d).start()
+
+    def fold3(m):
+        for d in (1, 3, 2):
+            swap3(m, d).wait()
+        total = jnp.zeros((16, D), F32)
+        for i in range(4):
+            total += r.r3[m, lax.rem(coord[orders[m][2]] - i + 4, 4)].astype(F32)
+        spot(m, 2)[...] = (total * scale).astype(BF16)
+        for d in (2, 1, 3):
+            ag(m, 2, d).start()
+
+    def spread(m, level):
+        for d in (1, 3, 2):
+            ag(m, level, d).wait()
+        if level == 2:
+            for d in (2, 1, 3):
+                ag(m, 1, d).start()
+        else:
+            ag_core(m).start()
+
+    def vec_copies(level):
+        if level == 0:
+            return [rcopy(r.vec.at[0], r.vrecv.at[0, 1], r.vs.at[0, 0], r.vr.at[0, 0], other)]
+        return [
+            rcopy(r.vec.at[level], r.vrecv.at[level, d], r.vs.at[level, d - 1], r.vr.at[level, d - 1], peer("xyz"[level - 1], d)[0])
+            for d in (1, 2, 3)
+        ]
+
+    def vec_step(level):
+        for q in vec_copies(level):
+            q.wait()
+        if level == 0:
+            total = r.vec[0] + r.vrecv[0, 1]
+        else:
+            r.vrecv[level, 0] = r.vec[level]
+            total = jnp.zeros((8, D), F32)
+            for i in range(4):
+                total += r.vrecv[level, lax.rem(coord["xyz"[level - 1]] - i + 4, 4)]
+        if level < 3:
+            r.vec[level + 1] = total
+            for q in vec_copies(level + 1):
+                q.start()
+        else:
+            r.vout[...] = total[0:4] * scale
+
     bar = pltpu.get_barrier_semaphore()
 
-    @pl.loop(1, DEVICES)
-    def _(k):
-        pl.semaphore_signal(bar, inc=1, device_id=dev(lax.rem(me + k, DEVICES)), device_id_type=MESH)
+    zs = [lax.rem(z + i, 4) for i in range(4)]
+    ys = [lax.rem(y + i, 4) * 8 for i in range(4)]
+    xs = [lax.rem(x + i, 4) * 2 for i in range(4)]
+    cores = [c, 1 - c]
+
+    def away(d):
+        return (zs[d[0]], ys[d[1]] + xs[d[2]] + cores[d[3]])
+
+    for d in ORDER:
+        pl.semaphore_signal(bar, inc=1, device_id=away(d), device_id_type=MESH)
 
     h, inv = norm_rows(r.lat[...].astype(F32))
     r.lhat[...] = h
@@ -190,10 +317,9 @@
     for q in halo:
         q.start()
 
-    @pl.loop(1, DEVICES)
-    def _(k):
-        t = lax.rem(me + k, DEVICES)
-        rcopy(r.pk.at[t], r.arr.at[me], r.as_, r.ar, dev(t)).start()
+    for d in ORDER:
+        t = away(d)
+        rcopy(r.pk.at[t[0] * 32 + t[1]], r.arr.at[me], r.as_, r.ar, t).start()
 
     r.arr[me] = r.pk[me]
 
@@ -251,11 +377,10 @@
     r.part[NODE_OUT] = mm_at(hidden, r.cot[...]).astype(BF16)
     r.part[NODE_SELF] = mm_at(own(), r.gnp[...]).astype(BF16)
 
-    def core_copy(p):
-        return rcopy(r.part.at[2 * p + 1 - c], r.crecv.at[p], r.cs.at[p], r.cr.at[p], at(z, y, x, 1 - c))
-
-    core_copy(0).start()
     r.part[NODE_AGG] = mm_at(r.aggr[...], r.gnp[...]).astype(BF16)
+    early, late = (NODE_OUT, NODE_SELF, NODE_AGG), (RECEIVE, EDGE, SEND)
+    for m in early:
+        core_copy(m).start()
 
     up = gagg * r.egain[...]
     r.npre[...] = up - mean_row(up)
@@ -272,27 +397,30 @@
         r.acc[...] += mm_at(r.act[k], g)
 
     pl.loop(DEG, EDGES)(edge_backward)
-
-    for j in range(4):
-        block = jnp.zeros((256, D), F32)
-        for k in range(CDEG):
-            block += mm(sub_hot(r.slot[k : k + 1, :] - 256 * j, 256), r.geb[DEG + k])
-        r.pk2[32 * j : 32 * j + 32] = to_pairs(block)
-
-    @pl.loop(1, DEVICES)
-    def _(k):
-        t = lax.rem(me + k, DEVICES)
-        rcopy(r.pk2.at[t], r.arr2.at[me], r.as2, r.ar2, dev(t)).start()
-
-    r.arr2[me] = r.pk2[me]
-
+    for m in early:
+        fold_core(m)
     pl.loop(0, DEG)(edge_backward)
+
     r.part[EDGE] = r.acc[...].astype(BF16)
+    core_copy(EDGE).start()
+    r.grecv[...] = r.recv[...].astype(BF16)
+    r.part[RECEIVE] = mm_at(own(), r.grecv[...]).astype(BF16)
+    core_copy(RECEIVE).start()
     for j in range(4):
         block = jnp.zeros((RIM, D), F32)
         for k in range(DEG):
             block += mm(sub_hot(r.near[k : k + 1, :] - RIM * j, RIM), r.geb[k])
         r.gext[RIM * j : RIM * j + RIM] = block
+    r.acc[...] = mm_at(r.ext_n[...], r.gext[...].astype(BF16))
+    for k in range(CDEG):
+        r.acc[...] += mm_at(r.cn[k], r.geb[DEG + k])
+    r.part[SEND] = r.acc[...].astype(BF16)
+    core_copy(SEND).start()
+    for m in early:
+        fold1(m)
+    for m in (EDGE, RECEIVE, SEND):
+        fold_core(m)
+
     r.rims[0] = r.gext[0:RIM].astype(BF16)
     r.rims[1] = r.gext[3 * RIM : 4 * RIM].astype(BF16)
     halo_back = [
@@ -301,152 +429,51 @@
     ]
     for q in halo_back:
         q.start()
-    r.vec[0, 1:2] = col_sum(r.recv[...])
-    r.grecv[...] = r.recv[...].astype(BF16)
-    r.part[RECEIVE] = mm_at(own(), r.grecv[...]).astype(BF16)
-    r.acc[...] = mm_at(r.ext_n[...], r.gext[...].astype(BF16))
-    for k in range(CDEG):
-        r.acc[...] += mm_at(r.cn[k], r.geb[DEG + k])
-    r.part[SEND] = r.acc[...].astype(BF16)
-    core_copy(1).start()
-    core_copy(2).start()
+    for j in range(4):
+        block = jnp.zeros((256, D), F32)
+        for k in range(CDEG):
+            block += mm(sub_hot(r.slot[k : k + 1, :] - 256 * j, 256), r.geb[DEG + k])
+        r.pk2[32 * j : 32 * j + 32] = to_pairs(block)
+    r.arr2[me] = r.pk2[me]
+
+    def send_back(first, last):
+        for d in ORDER[first:last]:
+            t = away(d)
+            rcopy(r.pk2.at[t[0] * 32 + t[1]], r.arr2.at[me], r.as2, r.ar2, t).start()
+
+    send_back(0, 32)
     local_back = mm_bt(r.gnp[...], r.ni[0:D]) + mm_bt(r.grecv[...], r.rw[...])
     r.gnb[...] = local_back
     through_sent = jnp.sum(r.sw[...].astype(F32) * r.acc[...], axis=1, keepdims=True)
     through_sent = jnp.transpose(jnp.broadcast_to(through_sent, (D, 128)))[0:1]
     r.vec[0, 0:1] = col_sum(r.lhat[...] * local_back) + through_sent / r.ngain[...]
-
-    orders = ("xyz", "yzx", "zxy")
-    scale = float(ROWS * DEVICES) ** -0.5
-
-    def rs1(p, d):
-        device, pos = peer(orders[p][0], d)
-        return rcopy(r.s1.at[p, pl.ds(pl.multiple_of(pos * 128, 128), 128)], r.r1.at[p, d - 1], r.s1s.at[p, d - 1], r.s1r.at[p, d - 1], device)
-
-    def rs2(p, d):
-        device, pos = peer(orders[p][1], d)
-        return rcopy(r.s2.at[p, pl.ds(pl.multiple_of(pos * 32, 32), 32)], r.r2.at[p, d - 1], r.s2s.at[p, d - 1], r.s2r.at[p, d - 1], device)
-
-    def rs3(p, d):
-        device, pos = peer(orders[p][2], d)
-        return rcopy(r.s3.at[p, :, pl.ds(pl.multiple_of(pos * 128, 128), 128)], r.r3.at[p, d - 1], r.s3s.at[p, d - 1], r.s3r.at[p, d - 1], device)
-
-    def spot(p, level):
-        a, b, e = (coord[axis] for axis in orders[p])
-        rows, lanes = a * 128 + b * 32, pl.ds(pl.multiple_of(e * 128, 128), 128)
-        if level == 3:
-            return r.res.at[2 * p + c, pl.ds(pl.multiple_of(rows, 32), 32), lanes]
-        if level == 2:
-            return r.res.at[2 * p + c, pl.ds(pl.multiple_of(rows, 32), 32)]
-        if level == 1:
-            return r.res.at[2 * p + c, pl.ds(pl.multiple_of(a * 128, 128), 128)]
-        return r.res.at[2 * p + c]
-
-    def ag(p, level, d):
-        ssem, rsem = {3: (r.g3s, r.g3r), 2: (r.g2s, r.g2r), 1: (r.g1s, r.g1r)}[level]
-        device, _ = peer(orders[p][level - 1], d)
-        return rcopy(spot(p, level), spot(p, level), ssem.at[p, d - 1], rsem.at[p, d - 1], device)
-
-    def ag_core(p):
-        return rcopy(spot(p, 0), spot(p, 0), r.gcs.at[p], r.gcr.at[p], at(z, y, x, 1 - c))
-
-    def vec_core():
-        return rcopy(r.vec.at[0], r.vrecv.at[0, 1], r.vs.at[0, 0], r.vr.at[0, 0], at(z, y, x, 1 - c))
-
-    def vec_ring(level, d):
-        axis = "xyz"[level - 1]
-        device, _ = peer(axis, d)
-        return rcopy(r.vec.at[level], r.vrecv.at[level, d], r.vs.at[level, d - 1], r.vr.at[level, d - 1], device)
-
-    def vec_sum(level):
-        axis = "xyz"[level - 1]
-        mine = coord[axis]
-        r.vrecv[level, 0] = r.vec[level]
-        total = jnp.zeros((8, D), F32)
-        for i in range(4):
-            total += r.vrecv[level, lax.rem(mine - i + 4, 4)]
-        return total
-
-    def vec_total(level):
-        if level == 0:
-            return r.vec[0] + r.vrecv[0, 1]
-        return vec_sum(level)
-
-    vec_core().start()
-
-    def fold_core(p):
-        core_copy(p).wait()
-
-        @pl.loop(0, 4)
-        def _(j):
-            rows = pl.ds(pl.multiple_of(j * 128, 128), 128)
-            r.s1[p, rows] = (r.part[2 * p + c, rows].astype(F32) + r.crecv[p, rows].astype(F32)).astype(BF16)
-
-        for d in (2, 1, 3):
-            rs1(p, d).start()
-
-    def fold1(p):
-        total = r.s1[p, pl.ds(pl.multiple_of(coord[orders[p][0]] * 128, 128), 128)].astype(F32)
-        for d in (1, 3, 2):
-            rs1(p, d).wait()
-            total += r.r1[p, d - 1].astype(F32)
-        r.s2[p] = total.astype(BF16)
-        for d in (2, 1, 3):
-            rs2(p, d).start()
-
-    def fold2(p):
-        total = r.s2[p, pl.ds(pl.multiple_of(coord[orders[p][1]] * 32, 32), 32)].astype(F32)
-        for d in (1, 3, 2):
-            rs2(p, d).wait()
-            total += r.r2[p, d - 1].astype(F32)
-        r.s3[p] = total.astype(BF16)
-        for d in (2, 1, 3):
-            rs3(p, d).start()
-
-    def fold3(p):
-        total = r.s3[p, :, pl.ds(pl.multiple_of(coord[orders[p][2]] * 128, 128), 128)].astype(F32)
-        for d in (1, 3, 2):
-            rs3(p, d).wait()
-            total += r.r3[p, d - 1].astype(F32)
-        spot(p, 3)[...] = (total * scale).astype(BF16)
-        for d in (2, 1, 3):
-            ag(p, 3, d).start()
-
-    def spread(p, level):
-        for d in (1, 3, 2):
-            ag(p, level, d).wait()
-        if level > 1:
-            for d in (2, 1, 3):
-                ag(p, level - 1, d).start()
-        else:
-            ag_core(p).start()
-
-    def vec_step(level):
-        if level == 0:
-            vec_core().wait()
-        else:
-            for d in (1, 2, 3):
-                vec_ring(level, d).wait()
-        total = vec_total(level)
-        if level < 3:
-            r.vec[level + 1] = total
-            for d in (1, 2, 3):
-                vec_ring(level + 1, d).start()
-        else:
-            r.vout[...] = total[0:4] * scale
-
-    for p in range(3):
-        fold_core(p)
+    r.vec[0, 1:2] = col_sum(r.recv[...])
+    for q in vec_copies(0):
+        q.start()
+
+    for m in early:
+        fold2(m)
     vec_step(0)
-    for p in range(3):
-        fold1(p)
+    send_back(32, 64)
+    for m in late:
+        fold1(m)
+    for m in early:
+        fold3(m)
+    send_back(64, 96)
     vec_step(1)
-    for p in range(3):
-        fold2(p)
+    for m in late:
+        fold2(m)
+    for m in early:
+        spread(m, 2)
+    send_back(96, 127)
     vec_step(2)
-    for p in range(3):
-        fold3(p)
+    for m in late:
+        fold3(m)
+    for m in early:
+        spread(m, 1)
     vec_step(3)
+    for m in late:
+        spread(m, 2)
 
     for q in halo_back:
         q.wait()
@@ -463,11 +490,18 @@
     back = r.linv[...] * (up - mean_row(up) - h * mean_row(up * h))
     r.glat[...] = (r.cot[...].astype(F32) + back).astype(BF16)
 
-    for level in (3, 2, 1):
-        for p in range(3):
-            spread(p, level)
-    for p in range(3):
-        ag_core(p).wait()
+    for m in late:
+        spread(m, 1)
+    for m in range(6):
+        ag_core(m).wait()
+
+
+def widen(sums, *outs):
+    for out, m in zip(outs, (SEND, RECEIVE, EDGE, NODE_SELF, NODE_OUT)):
+        if m == NODE_SELF:
+            out[...] = sums[m : m + 2].astype(F32)
+        else:
+            out[...] = sums[m].astype(F32)
 
 
 def per_device(
@@ -494,11 +528,18 @@
         edge_bias.reshape(1, D), edge_weight, edge_gain.reshape(1, D), node_input, node_bias.reshape(1, D),
         node_output, cotangent,
     )
-    wide = sums.astype(F32)
-    return (
-        new_latents, grad_latents, wide[SEND], wide[RECEIVE], wide[EDGE],
-        wide[NODE_SELF : NODE_AGG + 1].reshape(2 * D, D), wide[NODE_OUT], vectors,
-    )
+    rows = 128
+    square = pl.BlockSpec((rows, D), lambda i: (i, 0))
+    twice = pl.BlockSpec((2, rows, D), lambda i: (0, i, 0))
+    one = jax.ShapeDtypeStruct((D, D), F32)
+    send, receive, edge, node_in, node_out = pl.pallas_call(
+        widen,
+        grid=(D // rows,),
+        out_shape=(one, one, one, jax.ShapeDtypeStruct((2, D, D), F32), one),
+        in_specs=[pl.BlockSpec((6, rows, D), lambda i: (0, i, 0))],
+        out_specs=(square, square, square, twice, square),
+    )(sums)
+    return new_latents, grad_latents, send, receive, edge, node_in.reshape(2 * D, D), node_out, vectors
 
 
 def solution(mesh):

time: 95.5 us -> 85.9 us (0.90)
  local copies, waits for them, and re-layouts: 7.08 us -> 2.02 us
  Pallas kernels: 86.8 us -> 83 us
    pallas_call x1, Pallas kernels: 86.8 us -> 78.1 us  [per_device(): pl.pallas_call(body, out_shape=(jax.ShapeDtypeStruct((ROWS, D), BF16), ja...]
    pallas_call x0 -> x1, Pallas kernels: none -> 4.96 us  [per_device(): pl.pallas_call(widen, grid=(D // rows,), out_shape=(one, one, one, jax.Sh...]
    slice x1 -> x0, local copies, waits for them, and re-layouts: 2.99 us -> none  [per_device(): wide[NODE_SELF:NODE_AGG + 1].reshape(2 * D, D)]
    squeeze x1 -> x0, local copies, waits for them, and re-layouts: 2.08 us -> none  [per_device(): wide[NODE_OUT]]
    unnamed x11 -> x9, local copies, waits for them, and re-layouts: 2.02 us -> 2.02 us
where the time goes in v2:
time: 85.9 us; the launch traced here: 85.7 us
  Pallas kernels  83 us (97%)
  local copies, waits for them, and re-layouts  2.02 us (2%)
    pallas_call x1, Pallas kernels, per_device(): pl.pallas_call(body, out_shape=(jax.ShapeDtypeStruct((ROWS, D), BF16), ja...  78.1 us
    pallas_call x1, Pallas kernels, per_device(): pl.pallas_call(widen, grid=(D // rows,), out_shape=(one, one, one, jax.Sh...  4.96 us
    unnamed x9, local copies, waits for them, and re-layouts  2.02 us

profile of v2, /device:TPU:1, one launch (start us, length us, event | category | flops | bytes accessed | tf_op | source)
XLA Modules:
  0.0 85.7 jit_solution(7967217183675918149)
XLA Ops:
  0.6 78.1 %shard_map.197 = (bf16[256,512]{1,0:T(8,128)(2,1)}, bf16[256,512]{1,0:T(8,128)(2,1)}, bf16[6,512,512]{2,1,0:T(8,128)(2,1)}, f32[4,512]{1,0:T(4,128)}) custom-call(bf16[256,512]{1,0:T(8,128)(2,1)} %refs_0_.1, s32[4,256]{1,0:T(4,128)} %refs_1_.1, s32[2,256]{1,0:T(2,128)} %refs_2_.1, s32[1,1024]{1,0:T(1,128)} %refs_3_.1, f32[1,512]{1,0:T(1,128)} %bitcast.5, ...), custom_call_target="tpu_custom_call" | custom-call | tf_op jit(solution)/shard_map/pallas_call | solution.py:512
  78.7 0.0 copy-start.1
  78.7 0.0 copy-start
  78.8 0.0 copy-start.2
  78.8 5.0 %shard_map.198 = (f32[512,512]{1,0:T(8,128)}, f32[512,512]{1,0:T(8,128)}, f32[512,512]{1,0:T(8,128)}, f32[2,512,512]{2,1,0:T(8,128)}, f32[512,512]{1,0:T(8,128)}) custom-call(bf16[6,512,512]{2,1,0:T(8,128)(2,1)} %get-tuple-element.19.sums), custom_call_target="tpu_custom_call" | custom-call | tf_op jit(solution)/shard_map/pallas_call | solution.py:535
  83.7 0.0 copy-done.1
  83.7 0.7 copy.25
  84.4 0.0 copy-done
  84.4 0.7 copy.26
  85.1 0.0 copy-done.2
  85.1 0.6 copy.27
Async XLA Ops:
  78.7 5.0 %copy-start.1 = (bf16[256,512]{1,0:T(8,128)(2,1)S(1)}, bf16[256,512]{1,0:T(8,128)(2,1)}, u32[]{:S(2)}) copy-start(bf16[256,512]{1,0:T(8,128)(2,1)} %get-tuple-element.34) | copy-start | bytes 786436
  78.7 5.7 %copy-start = (bf16[256,512]{1,0:T(8,128)(2,1)S(1)}, bf16[256,512]{1,0:T(8,128)(2,1)}, u32[]{:S(2)}) copy-start(bf16[256,512]{1,0:T(8,128)(2,1)} %get-tuple-element.35) | copy-start | bytes 786436
  78.8 6.4 %copy-start.2 = (f32[4,512]{1,0:T(4,128)S(1)}, f32[4,512]{1,0:T(4,128)}, u32[]{:S(2)}) copy-start(f32[4,512]{1,0:T(4,128)} %get-tuple-element.41) | copy-start | bytes 24580

commit v3 on v2

--- a/solution.py
+++ b/solution.py
@@ -38,6 +38,7 @@
 
 
 ORDER = exchange_order()
+FIRST, SECOND, THIRD = 32, 64, 96
 
 
 def mm(a, b):
@@ -104,7 +105,23 @@
 def scratch():
     dma = pltpu.SemaphoreType.DMA
     half = (DEVICES, 2 * CAP, D // 2)
+    square = pltpu.VMEM((D, D), BF16)
+    row = pltpu.VMEM((1, D), F32)
     return {
+        "lat": pltpu.VMEM((ROWS, D), BF16),
+        "near": pltpu.VMEM((DEG, ROWS), jnp.int32),
+        "slot": pltpu.VMEM((CDEG, ROWS), jnp.int32),
+        "csend": pltpu.VMEM((1, SLOTS), jnp.int32),
+        "ngain": row, "sw": square, "rw": square, "ebias": row, "ew": square, "egain": row,
+        "ni": pltpu.VMEM((2 * D, D), BF16),
+        "nbias": row, "no": square,
+        "cot": pltpu.VMEM((ROWS, D), BF16),
+        "loads": dma((14,)),
+        "newlat": pltpu.VMEM((ROWS, D), BF16),
+        "glat": pltpu.VMEM((ROWS, D), BF16),
+        "res": pltpu.VMEM((6, D, D), BF16),
+        "vout": pltpu.VMEM((4, D), F32),
+        "stores": dma((15,)),
         "ext_n": pltpu.VMEM((ROWS + 2 * RIM, D), BF16),
         "lhat": pltpu.VMEM((ROWS, D), F32),
         "linv": pltpu.VMEM((ROWS, 1), F32),
@@ -152,7 +169,8 @@
 
 
 def body(*refs):
-    r = types.SimpleNamespace(**dict(zip(INPUTS + OUTPUTS + list(scratch()), refs)))
+    names = ["in_" + n for n in INPUTS] + ["out_" + n for n in OUTPUTS] + list(scratch())
+    r = types.SimpleNamespace(**dict(zip(names, refs)))
     la = lax.axis_index("lat")
     lo = lax.axis_index("lon")
     me = la * 32 + lo
@@ -253,6 +271,7 @@
                 ag(m, 1, d).start()
         else:
             ag_core(m).start()
+            store(r.res.at[m, half(c)], r.out_res.at[m, half(c)])
 
     def vec_copies(level):
         if level == 0:
@@ -278,6 +297,7 @@
                 q.start()
         else:
             r.vout[...] = total[0:4] * scale
+            store(r.vout, r.out_vout)
 
     bar = pltpu.get_barrier_semaphore()
 
@@ -291,6 +311,24 @@
 
     for d in ORDER:
         pl.semaphore_signal(bar, inc=1, device_id=away(d), device_id_type=MESH)
+
+    def load(name):
+        return pltpu.make_async_copy(getattr(r, "in_" + name), getattr(r, name), r.loads.at[INPUTS.index(name)])
+
+    def need(*wanted):
+        for name in wanted:
+            load(name).wait()
+
+    stores = []
+
+    def store(source, target):
+        copy = pltpu.make_async_copy(source, target, r.stores.at[len(stores)])
+        copy.start()
+        stores.append(copy)
+
+    for name in ("lat", "ngain", "csend", "near", "slot", "rw", "ebias", "sw", "cot", "no", "ni", "nbias", "ew", "egain"):
+        load(name).start()
+    need("lat", "ngain", "csend", "near", "slot")
 
     h, inv = norm_rows(r.lat[...].astype(F32))
     r.lhat[...] = h
@@ -322,6 +360,8 @@
         rcopy(r.pk.at[t[0] * 32 + t[1]], r.arr.at[me], r.as_, r.ar, t).start()
 
     r.arr[me] = r.pk[me]
+
+    need("rw", "ebias", "sw", "cot", "no", "ni", "nbias", "ew", "egain")
 
     def own():
         return r.ext_n[RIM : RIM + ROWS]
@@ -367,6 +407,7 @@
     hidden, node_slope = silu_parts(r.npre[...] + mm(aggregate, r.ni[D : 2 * D]))
     hidden = hidden.astype(BF16)
     r.newlat[...] = (r.lat[...].astype(F32) + mm(hidden, r.no[...])).astype(BF16)
+    store(r.newlat, r.out_newlat)
     gnp = (r.gh[...] * node_slope).astype(BF16)
     r.gnp[...] = gnp
     r.aggr[...] = aggregate
@@ -397,6 +438,19 @@
         r.acc[...] += mm_at(r.act[k], g)
 
     pl.loop(DEG, EDGES)(edge_backward)
+    for j in range(4):
+        block = jnp.zeros((256, D), F32)
+        for k in range(CDEG):
+            block += mm(sub_hot(r.slot[k : k + 1, :] - 256 * j, 256), r.geb[DEG + k])
+        r.pk2[32 * j : 32 * j + 32] = to_pairs(block)
+    r.arr2[me] = r.pk2[me]
+
+    def send_back(first, last):
+        for d in ORDER[first:last]:
+            t = away(d)
+            rcopy(r.pk2.at[t[0] * 32 + t[1]], r.arr2.at[me], r.as2, r.ar2, t).start()
+
+    send_back(0, FIRST)
     for m in early:
         fold_core(m)
     pl.loop(0, DEG)(edge_backward)
@@ -429,19 +483,6 @@
     ]
     for q in halo_back:
         q.start()
-    for j in range(4):
-        block = jnp.zeros((256, D), F32)
-        for k in range(CDEG):
-            block += mm(sub_hot(r.slot[k : k + 1, :] - 256 * j, 256), r.geb[DEG + k])
-        r.pk2[32 * j : 32 * j + 32] = to_pairs(block)
-    r.arr2[me] = r.pk2[me]
-
-    def send_back(first, last):
-        for d in ORDER[first:last]:
-            t = away(d)
-            rcopy(r.pk2.at[t[0] * 32 + t[1]], r.arr2.at[me], r.as2, r.ar2, t).start()
-
-    send_back(0, 32)
     local_back = mm_bt(r.gnp[...], r.ni[0:D]) + mm_bt(r.grecv[...], r.rw[...])
     r.gnb[...] = local_back
     through_sent = jnp.sum(r.sw[...].astype(F32) * r.acc[...], axis=1, keepdims=True)
@@ -454,18 +495,18 @@
     for m in early:
         fold2(m)
     vec_step(0)
-    send_back(32, 64)
+    send_back(FIRST, SECOND)
     for m in late:
         fold1(m)
     for m in early:
         fold3(m)
-    send_back(64, 96)
+    send_back(SECOND, THIRD)
     vec_step(1)
     for m in late:
         fold2(m)
     for m in early:
         spread(m, 2)
-    send_back(96, 127)
+    send_back(THIRD, DEVICES - 1)
     vec_step(2)
     for m in late:
         fold3(m)
@@ -489,26 +530,52 @@
     h = r.lhat[...]
     back = r.linv[...] * (up - mean_row(up) - h * mean_row(up * h))
     r.glat[...] = (r.cot[...].astype(F32) + back).astype(BF16)
+    store(r.glat, r.out_glat)
 
     for m in late:
         spread(m, 1)
     for m in range(6):
         ag_core(m).wait()
-
-
-def widen(sums, *outs):
-    for out, m in zip(outs, (SEND, RECEIVE, EDGE, NODE_SELF, NODE_OUT)):
-        if m == NODE_SELF:
-            out[...] = sums[m : m + 2].astype(F32)
-        else:
-            out[...] = sums[m].astype(F32)
+        store(r.res.at[m, half(1 - c)], r.out_res.at[m, half(1 - c)])
+    for copy in stores:
+        copy.wait()
+
+
+def widen(sums, newlat, glat, vectors, *refs):
+    outs, narrow, wide, rows, vec, in_sems, out_sems = refs[:8], *refs[8:]
+    loads = [pltpu.make_async_copy(sums.at[m], narrow.at[m], in_sems.at[m]) for m in range(6)]
+    through = ((newlat, rows.at[0], outs[0]), (glat, rows.at[1], outs[1]), (vectors, vec, outs[7]))
+    for i, (source, held, _) in enumerate(through):
+        loads.append(pltpu.make_async_copy(source, held, in_sems.at[6 + i]))
+    for copy in loads:
+        copy.start()
+    stores = []
+
+    def store(source, target):
+        copy = pltpu.make_async_copy(source, target, out_sems.at[len(stores)])
+        copy.start()
+        stores.append(copy)
+
+    targets = {
+        SEND: outs[2], RECEIVE: outs[3], EDGE: outs[4], NODE_OUT: outs[6],
+        NODE_SELF: outs[5].at[pl.ds(0, D)], NODE_AGG: outs[5].at[pl.ds(D, D)],
+    }
+    for m in range(6):
+        loads[m].wait()
+        wide[m] = narrow[m].astype(F32)
+        store(wide.at[m], targets[m])
+    for i, (_, held, target) in enumerate(through):
+        loads[6 + i].wait()
+        store(held, target)
+    for copy in stores:
+        copy.wait()
 
 
 def per_device(
     latents, near_index, coarse_slot, coarse_send, norm_gain, send_weight, receive_weight, edge_bias,
     edge_weight, edge_gain, node_input, node_bias, node_output, cotangent,
 ):
-    whole = pl.BlockSpec(memory_space=pltpu.VMEM)
+    whole = pl.BlockSpec(memory_space=pltpu.HBM)
     new_latents, grad_latents, sums, vectors = pl.pallas_call(
         body,
         out_shape=(
@@ -528,18 +595,22 @@
         edge_bias.reshape(1, D), edge_weight, edge_gain.reshape(1, D), node_input, node_bias.reshape(1, D),
         node_output, cotangent,
     )
-    rows = 128
-    square = pl.BlockSpec((rows, D), lambda i: (i, 0))
-    twice = pl.BlockSpec((2, rows, D), lambda i: (0, i, 0))
-    one = jax.ShapeDtypeStruct((D, D), F32)
-    send, receive, edge, node_in, node_out = pl.pallas_call(
+    shard, one = jax.ShapeDtypeStruct((ROWS, D), BF16), jax.ShapeDtypeStruct((D, D), F32)
+    return pl.pallas_call(
         widen,
-        grid=(D // rows,),
-        out_shape=(one, one, one, jax.ShapeDtypeStruct((2, D, D), F32), one),
-        in_specs=[pl.BlockSpec((6, rows, D), lambda i: (0, i, 0))],
-        out_specs=(square, square, square, twice, square),
-    )(sums)
-    return new_latents, grad_latents, send, receive, edge, node_in.reshape(2 * D, D), node_out, vectors
+        out_shape=(
+            shard, shard, one, one, one, jax.ShapeDtypeStruct((2 * D, D), F32), one,
+            jax.ShapeDtypeStruct((4, D), F32),
+        ),
+        in_specs=[whole] * 4,
+        out_specs=(whole,) * 8,
+        scratch_shapes=[
+            pltpu.VMEM((6, D, D), BF16), pltpu.VMEM((6, D, D), F32),
+            pltpu.VMEM((2, ROWS, D), BF16), pltpu.VMEM((4, D), F32),
+            pltpu.SemaphoreType.DMA((9,)), pltpu.SemaphoreType.DMA((9,)),
+        ],
+        compiler_params=pltpu.CompilerParams(vmem_limit_bytes=58 * 2**20),
+    )(sums, new_latents, grad_latents, vectors)
 
 
 def solution(mesh):

time: 85.9 us -> 78.1 us (0.909)
  Pallas kernels: 83 us -> 77.4 us
  local copies, waits for them, and re-layouts: 2.02 us -> 0 us
    pallas_call x1, Pallas kernels: 78.1 us -> 73.3 us  [per_device(): pl.pallas_call(body, out_shape=(jax.ShapeDtypeStruct((ROWS, D), BF16), ja...]
    unnamed x9 -> x0, local copies, waits for them, and re-layouts: 2.02 us -> none
    pallas_call x1, Pallas kernels: 4.96 us -> 4.06 us  [per_device(): pl.pallas_call(widen, out_shape=(shard, shard, one, one, one, jax.ShapeDt...]
where the time goes in v3:
time: 78.1 us; the launch traced here: 78 us
  Pallas kernels  77.4 us (99%)
    pallas_call x1, Pallas kernels, per_device(): pl.pallas_call(body, out_shape=(jax.ShapeDtypeStruct((ROWS, D), BF16), ja...  73.3 us
    pallas_call x1, Pallas kernels, per_device(): pl.pallas_call(widen, out_shape=(shard, shard, one, one, one, jax.ShapeDt...  4.06 us

profile of v3, /device:TPU:1, one launch (start us, length us, event | category | flops | bytes accessed | tf_op | source)
XLA Modules:
  0.0 78.0 jit_solution(14977491960611060328)
XLA Ops:
  0.6 73.3 %shard_map.197 = (bf16[256,512]{1,0:T(8,128)(2,1)}, bf16[256,512]{1,0:T(8,128)(2,1)}, bf16[6,512,512]{2,1,0:T(8,128)(2,1)}, f32[4,512]{1,0:T(4,128)}) custom-call(bf16[256,512]{1,0:T(8,128)(2,1)} %refs_0_.1, s32[4,256]{1,0:T(4,128)} %refs_1_.1, s32[2,256]{1,0:T(2,128)} %refs_2_.1, s32[1,1024]{1,0:T(1,128)} %refs_3_.1, f32[1,512]{1,0:T(1,128)} %bitcast.4, ...), custom_call_target="tpu_custom_call" | custom-call | tf_op jit(solution)/shard_map/pallas_call | solution.py:579
  73.9 4.1 %shard_map.198 = (bf16[256,512]{1,0:T(8,128)(2,1)}, bf16[256,512]{1,0:T(8,128)(2,1)}, f32[512,512]{1,0:T(8,128)}, f32[512,512]{1,0:T(8,128)}, f32[512,512]{1,0:T...) custom-call(bf16[6,512,512]{2,1,0:T(8,128)(2,1)} %get-tuple-element.12.sums, ...), custom_call_target="tpu_custom_call" | custom-call | tf_op jit(solution)/shard_map/pallas_call | solution.py:599

commit v4 on v3

--- a/solution.py
+++ b/solution.py
@@ -18,6 +18,7 @@
 DEVICES = 128
 CAP = 8
 SLOTS = DEVICES * CAP
+EXT = ROWS + 2 * RIM
 F32 = jnp.float32
 BF16 = jnp.bfloat16
 
@@ -38,7 +39,7 @@
 
 
 ORDER = exchange_order()
-FIRST, SECOND, THIRD = 32, 64, 96
+FIRST, SECOND, THIRD = 64, 85, 106
 
 
 def mm(a, b):
@@ -122,7 +123,7 @@
         "res": pltpu.VMEM((6, D, D), BF16),
         "vout": pltpu.VMEM((4, D), F32),
         "stores": dma((15,)),
-        "ext_n": pltpu.VMEM((ROWS + 2 * RIM, D), BF16),
+        "ext_n": pltpu.VMEM((EXT + CDEG * ROWS, D), BF16),
         "lhat": pltpu.VMEM((ROWS, D), F32),
         "linv": pltpu.VMEM((ROWS, 1), F32),
         "pk": pltpu.VMEM(half, BF16),
@@ -140,11 +141,13 @@
         "hat": pltpu.VMEM((EDGES, ROWS, D), F32),
         "einv": pltpu.VMEM((EDGES, ROWS, 1), F32),
         "hsum": pltpu.VMEM((ROWS, D), F32),
-        "cn": pltpu.VMEM((CDEG, ROWS, D), BF16),
-        "geb": pltpu.VMEM((EDGES, ROWS, D), BF16),
+        "gsend": pltpu.VMEM((EXT + CDEG * ROWS, D), BF16),
+        "gpre": pltpu.VMEM((EDGES, ROWS, D), BF16),
+        "geb": pltpu.VMEM((DEG, ROWS, D), BF16),
         "gext": pltpu.VMEM((ROWS + 2 * RIM, D), F32),
-        "rims": pltpu.VMEM((4, RIM, D), BF16),
+        "rims": pltpu.VMEM((2, RIM, D), BF16),
         "gnp": pltpu.VMEM((ROWS, D), BF16),
+        "hidden": pltpu.VMEM((ROWS, D), BF16),
         "aggr": pltpu.VMEM((ROWS, D), BF16),
         "grecv": pltpu.VMEM((ROWS, D), BF16),
         "gnb": pltpu.VMEM((ROWS, D), F32),
@@ -400,14 +403,13 @@
     @pl.loop(0, CDEG)
     def _(k):
         rows = mm(lane_hot(r.cols[DEG + k], SLOTS), r.arr_n[...]).astype(BF16)
-        r.cn[k] = rows
+        r.ext_n[pl.ds(pl.multiple_of(EXT + k * ROWS, ROWS), ROWS)] = rows
         edge_forward(DEG + k, mm(rows, r.sw[...]).astype(BF16).astype(F32))
 
     aggregate = (r.hsum[...] * r.egain[...]).astype(BF16)
     hidden, node_slope = silu_parts(r.npre[...] + mm(aggregate, r.ni[D : 2 * D]))
     hidden = hidden.astype(BF16)
-    r.newlat[...] = (r.lat[...].astype(F32) + mm(hidden, r.no[...])).astype(BF16)
-    store(r.newlat, r.out_newlat)
+    r.hidden[...] = hidden
     gnp = (r.gh[...] * node_slope).astype(BF16)
     r.gnp[...] = gnp
     r.aggr[...] = aggregate
@@ -415,7 +417,7 @@
     r.vec[0] = jnp.zeros((8, D), F32)
     r.vec[0, 2:3] = col_sum(gagg * r.hsum[...])
     r.vec[0, 3:4] = col_sum(gnp.astype(F32))
-    r.part[NODE_OUT] = mm_at(hidden, r.cot[...]).astype(BF16)
+    r.part[NODE_OUT] = mm_at(r.hidden[...], r.cot[...]).astype(BF16)
     r.part[NODE_SELF] = mm_at(own(), r.gnp[...]).astype(BF16)
 
     r.part[NODE_AGG] = mm_at(r.aggr[...], r.gnp[...]).astype(BF16)
@@ -426,22 +428,24 @@
     up = gagg * r.egain[...]
     r.npre[...] = up - mean_row(up)
     r.gh[...] = up
-    r.recv[...] = jnp.zeros((ROWS, D), F32)
-    r.acc[...] = jnp.zeros((D, D), F32)
 
     def edge_backward(k):
         h = r.hat[k]
         g = (r.einv[k] * (r.npre[...] - h * mean_row(r.gh[...] * h))).astype(BF16)
         ge = mm_bt(g, r.ew[...]) * r.slope[k]
-        r.recv[...] += ge
-        r.geb[k] = ge.astype(BF16)
-        r.acc[...] += mm_at(r.act[k], g)
-
-    pl.loop(DEG, EDGES)(edge_backward)
+        r.gpre[k] = g
+        return ge
+
+    total = jnp.zeros((ROWS, D), F32)
+    for k in range(CDEG):
+        ge = edge_backward(DEG + k)
+        total += ge
+        r.gsend[EXT + k * ROWS : EXT + (k + 1) * ROWS] = ge.astype(BF16)
+    r.recv[...] = total
     for j in range(4):
         block = jnp.zeros((256, D), F32)
         for k in range(CDEG):
-            block += mm(sub_hot(r.slot[k : k + 1, :] - 256 * j, 256), r.geb[DEG + k])
+            block += mm(sub_hot(r.slot[k : k + 1, :] - 256 * j, 256), r.gsend[EXT + k * ROWS : EXT + (k + 1) * ROWS])
         r.pk2[32 * j : 32 * j + 32] = to_pairs(block)
     r.arr2[me] = r.pk2[me]
 
@@ -453,9 +457,16 @@
     send_back(0, FIRST)
     for m in early:
         fold_core(m)
-    pl.loop(0, DEG)(edge_backward)
-
-    r.part[EDGE] = r.acc[...].astype(BF16)
+
+    @pl.loop(0, DEG, step=2)
+    def _(k):
+        one, two = edge_backward(k), edge_backward(k + 1)
+        r.geb[k] = one.astype(BF16)
+        r.geb[k + 1] = two.astype(BF16)
+        r.recv[...] += one + two
+
+    flat = (EDGES * ROWS, D)
+    r.part[EDGE] = mm_at(r.act[...].reshape(flat), r.gpre[...].reshape(flat)).astype(BF16)
     core_copy(EDGE).start()
     r.grecv[...] = r.recv[...].astype(BF16)
     r.part[RECEIVE] = mm_at(own(), r.grecv[...]).astype(BF16)
@@ -465,9 +476,8 @@
         for k in range(DEG):
             block += mm(sub_hot(r.near[k : k + 1, :] - RIM * j, RIM), r.geb[k])
         r.gext[RIM * j : RIM * j + RIM] = block
-    r.acc[...] = mm_at(r.ext_n[...], r.gext[...].astype(BF16))
-    for k in range(CDEG):
-        r.acc[...] += mm_at(r.cn[k], r.geb[DEG + k])
+        r.gsend[RIM * j : RIM * j + RIM] = block.astype(BF16)
+    r.acc[...] = mm_at(r.ext_n[...], r.gsend[...])
     r.part[SEND] = r.acc[...].astype(BF16)
     core_copy(SEND).start()
     for m in early:
@@ -475,11 +485,9 @@
     for m in (EDGE, RECEIVE, SEND):
         fold_core(m)
 
-    r.rims[0] = r.gext[0:RIM].astype(BF16)
-    r.rims[1] = r.gext[3 * RIM : 4 * RIM].astype(BF16)
     halo_back = [
-        rcopy(r.rims.at[1], r.rims.at[2], r.hs2.at[0], r.hr2.at[0], east),
-        rcopy(r.rims.at[0], r.rims.at[3], r.hs2.at[1], r.hr2.at[1], west),
+        rcopy(r.gsend.at[pl.ds(3 * RIM, RIM)], r.rims.at[0], r.hs2.at[0], r.hr2.at[0], east),
+        rcopy(r.gsend.at[pl.ds(0, RIM)], r.rims.at[1], r.hs2.at[1], r.hr2.at[1], west),
     ]
     for q in halo_back:
         q.start()
@@ -492,33 +500,35 @@
     for q in vec_copies(0):
         q.start()
 
+    for m in late:
+        fold1(m)
     for m in early:
         fold2(m)
+    r.newlat[...] = (r.lat[...].astype(F32) + mm(r.hidden[...], r.no[...])).astype(BF16)
+    store(r.newlat, r.out_newlat)
     vec_step(0)
     send_back(FIRST, SECOND)
     for m in late:
-        fold1(m)
+        fold2(m)
     for m in early:
         fold3(m)
+    vec_step(1)
     send_back(SECOND, THIRD)
-    vec_step(1)
     for m in late:
-        fold2(m)
+        fold3(m)
     for m in early:
         spread(m, 2)
     send_back(THIRD, DEVICES - 1)
     vec_step(2)
     for m in late:
-        fold3(m)
+        spread(m, 2)
     for m in early:
         spread(m, 1)
     vec_step(3)
-    for m in late:
-        spread(m, 2)
 
     for q in halo_back:
         q.wait()
-    grad_sent = r.gext[RIM : RIM + ROWS] + r.rims[2:4].reshape(ROWS, D).astype(F32)
+    grad_sent = r.gext[RIM : RIM + ROWS] + r.rims[...].reshape(ROWS, D).astype(F32)
     rcopy(r.pk2.at[pl.ds(0, DEVICES - 1)], r.arr2.at[pl.ds(0, DEVICES - 1)], r.as2, r.ar2, west).wait()
 
     @pl.loop(0, 8)

time: 78.1 us -> 77.7 us (level)
  no operation moved by 1% of the time
where the time goes in v4:
time: 77.7 us; the launch traced here: 77.6 us
  Pallas kernels  76.8 us (99%)
  between operations  0.81 us (1%)
    pallas_call x1, Pallas kernels, per_device(): pl.pallas_call(body, out_shape=(jax.ShapeDtypeStruct((ROWS, D), BF16), ja...  72.7 us
    pallas_call x1, Pallas kernels, per_device(): pl.pallas_call(widen, out_shape=(shard, shard, one, one, one, jax.ShapeDt...  4.06 us

profile of v4, /device:TPU:1, one launch (start us, length us, event | category | flops | bytes accessed | tf_op | source)
XLA Modules:
  0.0 77.6 jit_solution(14124817388019739049)
XLA Ops:
  0.6 72.7 %shard_map.197 = (bf16[256,512]{1,0:T(8,128)(2,1)}, bf16[256,512]{1,0:T(8,128)(2,1)}, bf16[6,512,512]{2,1,0:T(8,128)(2,1)}, f32[4,512]{1,0:T(4,128)}) custom-call(bf16[256,512]{1,0:T(8,128)(2,1)} %refs_0_.1, s32[4,256]{1,0:T(4,128)} %refs_1_.1, s32[2,256]{1,0:T(2,128)} %refs_2_.1, s32[1,1024]{1,0:T(1,128)} %refs_3_.1, f32[1,512]{1,0:T(1,128)} %bitcast.4, ...), custom_call_target="tpu_custom_call" | custom-call | tf_op jit(solution)/shard_map/pallas_call | solution.py:589
  73.4 4.1 %shard_map.198 = (bf16[256,512]{1,0:T(8,128)(2,1)}, bf16[256,512]{1,0:T(8,128)(2,1)}, f32[512,512]{1,0:T(8,128)}, f32[512,512]{1,0:T(8,128)}, f32[512,512]{1,0:T...) custom-call(bf16[6,512,512]{2,1,0:T(8,128)(2,1)} %get-tuple-element.12.sums, ...), custom_call_target="tpu_custom_call" | custom-call | tf_op jit(solution)/shard_map/pallas_call | solution.py:609
